TPU v7x, 32 devices: a whole 2x2x4 slice. The times are simulated.
32 devices in a mesh: grp: 4 (over x, core), tile: 8 (over z, y).
Axes of the slice: x: 2, y: 2, z: 4, core: 2. Of those that a mesh axis runs over, the one named last changes fastest.
Arguments:
- start_velocity: float32 [2, 128, 4096], P(None, 'grp', 'tile'), may hold values from -6 to 6
- driving_stress: float32 [2, 128, 4096], P(None, 'grp', 'tile'), may hold values from -6 to 6
- viscosity: float32 [2, 128, 4096], P(None, 'grp', 'tile'), may hold values from 0.3 to 3
- friction: float32 [128, 4096], P('grp', 'tile'), may hold values from 0.02 to 0.5
- cell_element: int32 [128, 4096], P('grp', 'tile'), may hold values from 0 to 4095, as said below
- observed: float32 [16384, 256], P(('grp', 'tile')), may hold values from -6 to 6
- look: float32 [2, 16384, 256], P(None, ('grp', 'tile')), may hold values from -3 to 3
- row_owner: int32 [16384, 1], P(('grp', 'tile')), may hold values from 0 to 31; in each aligned block of 512 rows (0 to 511, 512 to 1023, ...) at most 32 rows name the same one
- row_cell: int32 [16384], P(('grp', 'tile')), may hold values from 0 to 16383
Outputs:
- stress_adjoint: float32 [2, 128, 4096], P(None, 'grp', 'tile')
- friction_adjoint: float32 [4096], P(('grp', 'tile'))
Inputs may be any that keep to these rules, and one draw needn't show every extreme that they name: `row_owner`: of the 512 rows of one device at most 32 name the same owner, and in some blocks one owner is named by exactly 32 rows. `cell_element`: the element of a node held by the device with grp index g lies in g * 128 * 8 to (g + 1) * 128 * 8 - 1; element e is owned by the device at flattened index e // 128.
All inputs are finite; a program needn't handle non-finite values.
Results may differ from a plain program's by a relative error of at most 0.00002.
Values sent between devices are 32-bit elements; how exact they have to be, the bound alone decides.
No kernel may reach another device: no remote copies, remote signals or barrier semaphores. Data moves between devices by JAX's collectives and lax.ppermute only.
A program may use at most 128 MiB of HBM per device.

v0:
```python
import math

import jax
import jax.numpy as jnp
from jax import lax
from jax.sharding import PartitionSpec as P

SWEEPS = 8
PICARD = 2


def padded_2(block, sides, width):
    for axis, dim in sides:
        count = lax.axis_size(axis)
        forward = [(i, i + 1) for i in range(count - 1)]
        backward = [(target, source) for source, target in forward]
        low = lax.ppermute(
            lax.slice_in_dim(block, block.shape[dim] - width, None, axis=dim), axis, forward
        )
        high = lax.ppermute(lax.slice_in_dim(block, 0, width, axis=dim), axis, backward)
        block = jnp.concatenate([low, block, high], axis=dim)
    return block


def grad_x(p):
    return 0.5 * (p[1:, 1:] + p[1:, :-1] - p[:-1, 1:] - p[:-1, :-1])


def grad_y(p):
    return 0.5 * (p[1:, 1:] + p[:-1, 1:] - p[1:, :-1] - p[:-1, :-1])


def spread_x(t):
    return 0.5 * (t[:-1, :-1] + t[:-1, 1:] - t[1:, :-1] - t[1:, 1:])


def spread_y(t):
    return 0.5 * (t[:-1, :-1] + t[1:, :-1] - t[:-1, 1:] - t[1:, 1:])


def corner_mean(e):
    return 0.25 * (e[1:, 1:] + e[1:, :-1] + e[:-1, 1:] + e[:-1, :-1])


def local_operate(padded, quad_visc, friction):
    values = padded[:, 1:-1, 1:-1]
    u_dx = grad_x(padded[0])
    u_dy = grad_y(padded[0])
    v_dx = grad_x(padded[1])
    v_dy = grad_y(padded[1])
    stress_xx = quad_visc * (4.0 * u_dx + 2.0 * v_dy)
    stress_yy = quad_visc * (4.0 * v_dy + 2.0 * u_dx)
    stress_xy = quad_visc * (u_dy + v_dx)
    first = spread_x(stress_xx) + spread_y(stress_xy) + friction * values[0]
    second = spread_y(stress_yy) + spread_x(stress_xy) + friction * values[1]
    return jnp.stack([first, second])


def operate(values, quad_visc, friction):
    padded = padded_2(values, (("grp", 1), ("tile", 2)), 1)
    return local_operate(padded, quad_visc, friction)


def row_gradient(look_x, look_y, observed, speed_x, speed_y, epochs):
    misfit_rows = look_x * speed_x[:, None] + look_y * speed_y[:, None] - observed
    first = jnp.sum(misfit_rows * look_x, axis=1)
    second = jnp.sum(misfit_rows * look_y, axis=1)
    return jnp.stack([first, second]) / math.sqrt(epochs)


def shards(
    start_velocity,
    driving_stress,
    viscosity,
    friction,
    cell_element,
    observed,
    look,
    row_owner,
    row_cell,
):
    rows_x, rows_y = friction.shape
    row_dev, epochs = observed.shape
    devices = lax.axis_size("grp") * lax.axis_size("tile")
    capacity = max(2, 2 * row_dev // devices)
    owner_dev = row_owner[:, 0]
    owner_marks = (owner_dev[:, None] == jnp.arange(devices, dtype=jnp.int32)[None, :]).astype(
        jnp.int32
    )
    slot_rank = jnp.sum((jnp.cumsum(owner_marks, axis=0) - owner_marks) * owner_marks, axis=1)
    row_slot = owner_dev * capacity + slot_rank
    slot_cells = (
        jnp.zeros((devices * capacity,), jnp.int32)
        .at[row_slot]
        .set(row_cell)
        .reshape(devices, capacity)
    )
    packed = jnp.concatenate([look, observed[None]], axis=0)
    outgoing = jnp.zeros((3, devices * capacity, epochs), jnp.float32).at[:, row_slot].set(packed)
    arrived = lax.all_to_all(
        outgoing.reshape(3, devices, capacity, epochs),
        ("grp", "tile"),
        split_axis=1,
        concat_axis=1,
        tiled=True,
    )
    arrived = arrived.reshape(3, devices * capacity, epochs)
    arrived_cells = lax.all_to_all(
        slot_cells, ("grp", "tile"), split_axis=0, concat_axis=0, tiled=True
    ).reshape(-1)
    saved = []
    prec_list = []
    diag_list = []
    visc_rim = padded_2(viscosity, (("grp", 1), ("tile", 2)), 1)
    quad_list = []
    for picard in range(PICARD):
        quad_visc = corner_mean(visc_rim[picard])
        diagonal = (
            1.25
            * (quad_visc[:-1, :-1] + quad_visc[:-1, 1:] + quad_visc[1:, :-1] + quad_visc[1:, 1:])
            + friction
        )
        quad_list.append(quad_visc)
        diag_list.append(diagonal)
        prec_list.append(0.45 / diagonal)
    velocity = start_velocity
    for picard in range(PICARD):
        for _ in range(SWEEPS):
            residual = driving_stress - operate(velocity, quad_list[picard], friction)
            saved.append((velocity, residual))
            velocity = velocity + prec_list[picard] * residual
    flat_velocity = velocity.reshape(2, rows_x * rows_y)
    speeds = flat_velocity[:, arrived_cells]
    row_grads = row_gradient(arrived[0], arrived[1], arrived[2], speeds[0], speeds[1], epochs)
    adjoint = jnp.zeros((2, rows_x * rows_y), jnp.float32).at[:, arrived_cells].add(row_grads)
    adjoint = adjoint.reshape(2, rows_x, rows_y)
    stress_adjoint = jnp.zeros_like(driving_stress)
    friction_grad = jnp.zeros_like(friction)
    for position in range(len(saved) - 1, -1, -1):
        velocity_in, residual = saved[position]
        picard = position // SWEEPS
        precond = prec_list[picard]
        scaled = precond * adjoint
        stress_adjoint = stress_adjoint + scaled
        friction_grad = friction_grad - (scaled[0] * velocity_in[0] + scaled[1] * velocity_in[1])
        friction_grad = friction_grad - precond / diag_list[picard] * (
            adjoint[0] * residual[0] + adjoint[1] * residual[1]
        )
        if position > 0:
            adjoint = adjoint - operate(scaled, quad_list[picard], friction)
    node_terms = (friction * friction_grad).reshape(-1)
    elem_dev = rows_x * rows_y // 128
    group_width = elem_dev * lax.axis_size("tile")
    first_element = lax.axis_index("grp") * group_width
    local_ids = cell_element.reshape(-1) - first_element
    element_terms = jnp.zeros((group_width,), jnp.float32).at[local_ids].add(node_terms)
    friction_adjoint = lax.psum_scatter(element_terms, "tile", scatter_dimension=0, tiled=True)
    return (stress_adjoint, friction_adjoint)


def solution(mesh):
    return jax.shard_map(
        shards,
        mesh=mesh,
        in_specs=(
            P(None, "grp", "tile"),
            P(None, "grp", "tile"),
            P(None, "grp", "tile"),
            P("grp", "tile"),
            P("grp", "tile"),
            P(("grp", "tile"), None),
            P(None, ("grp", "tile"), None),
            P(("grp", "tile"), None),
            P(("grp", "tile")),
        ),
        out_specs=(P(None, "grp", "tile"), P(("grp", "tile"))),
        check_vma=False,
    )
```

profile of v0, /device:TPU:0, one launch (start us, length us, event | category | flops | bytes accessed | tf_op | source)
XLA Modules:
  0.0 849.3 jit_solution(4114822612060280438)
XLA Ops:
  5.9 5.1 collective-permute-start
  18.9 4.5 collective-permute-start.2
  37.6 4.7 collective-permute-done.9
  42.4 4.8 collective-permute-start.10
  48.9 4.2 collective-permute-done.11
  66.0 4.2 collective-permute-done.15
  78.5 4.8 collective-permute-start.18
  102.1 4.2 collective-permute-done.23
  114.6 4.8 collective-permute-start.26
  207.0 4.2 collective-permute-done.47
  227.1 4.9 all-to-all-start
  240.3 4.3 collective-permute-start.54
  248.5 47.5 %scatter_fusion = f32[3,1024,256]{2,0,1:T(4,128)} fusion(f32[3,1024,256]{2,0,1:T(4,128)} %broadcast_in_dim.11, s32[512]{0:T(512)} %bitcast.864, f32[512,3,256]{2,1,0:T(4,128)S(1)} %copy.22), kind=kCustom, calls=%fused_computation.2 | custom fusion | bytes 4720640 | tf_op jit(solution)/shard_map/scatter | solution.py:99
  296.0 4.4 copy.23
  301.7 8.3 all-to-all-start.1
  321.9 6.0 collective-permute-done.58
  330.6 17.3 %collective-permute-start.60 = (f32[2,1,512]{2,1,0:T(1,128)S(1)}, f32[2,1,512]{2,1,0:T(1,128)S(1)}, u32[]{:S(2)}, u32[]{:S(2)}) collective-permute-start(f32[2,1,512]{2,1,0:T(1,128)S(1)} %get-tuple-element.421), channel_id=1, source_target_pairs={{0,8},{8,16},{16,24},{1,9},{9,17},{17,25},{2,10},{10,18},{18,26},{... | collective-permute-start | bytes 12296 | tf_op jit(solution)/shard_map/ppermute | solution.py:17
  351.1 23.3 %collective-permute-start.62 = (f32[2,34,1]{2,1,0:T(8,128)S(1)}, f32[2,34,1]{2,1,0:T(8,128)S(1)}, u32[]{:S(2)}, u32[]{:S(2)}) collective-permute-start(f32[2,34,1]{2,1,0:T(8,128)S(1)} %get-tuple-element.357), channel_id=1, source_target_pairs={{0,1},{1,2},{2,3},{3,4},{4,5},{5,6},{6,7},{8,9},{9,10},{10,11},{11... | collective-permute-start | bytes 824 | tf_op jit(solution)/shard_map/ppermute | solution.py:17
  377.7 5.7 collective-permute-done.63
  390.6 18.3 %collective-permute-start.66 = (f32[2,34,1]{2,1,0:T(8,128)S(1)}, f32[2,34,1]{2,1,0:T(8,128)S(1)}, u32[]{:S(2)}, u32[]{:S(2)}) collective-permute-start(f32[2,34,1]{2,1,0:T(8,128)S(1)} %get-tuple-element.355), channel_id=1, source_target_pairs={{0,1},{1,2},{2,3},{3,4},{4,5},{5,6},{6,7},{8,9},{9,10},{10,11},{11... | collective-permute-start | bytes 824 | tf_op jit(solution)/shard_map/ppermute | solution.py:17
  410.6 4.2 collective-permute-done.67
  416.1 4.7 copy.24
  420.9 6.2 gather_fusion
  430.6 9.8 %scatter_custom_fusion.2 = f32[2,16384]{0,1:T(8,128)} fusion(s32[1024]{0:T(1024)S(1)} %bitcast.862, f32[1024,2]{1,0:T(8,128)S(1)} %copy.25, f32[]{:T(128)} %constant.158.clone.1), kind=kCustom, calls=%fused_computation.7 | custom fusion | flops 2048 | bytes 131076 | tf_op jit(solution)/shard_map/scatter-add | solution.py:135
  440.5 5.2 copy.26
  452.7 5.2 collective-permute-start.70
  459.6 4.2 collective-permute-done.71
  471.4 4.5 collective-permute-start.74
  494.0 4.2 collective-permute-done.79
  685.8 13.1 %slice_reduce_fusion.1 = (f32[16384]{0:T(1024)}, f32[16384]{0:T(1024)S(1)}) fusion(f32[2,16384]{0,1:T(8,128)} %scatter_custom_fusion.2), kind=kLoop, calls=%fused_computation.6 | loop fusion | bytes 262144 | tf_op jit(solution)/shard_map/slice | solution.py:147
  716.7 113.7 %scatter_custom_fusion.3 = f32[1024]{0:T(1024)S(1)} fusion(s32[16384]{0:T(1024)} %bitcast.857, f32[16384]{0:T(1024)S(1)} %bitcast.858, f32[]{:T(128)} %constant.158.clone.1), kind=kCustom, calls=%fused_computation.1077 | custom fusion | flops 16384 | bytes 4608 | tf_op jit(solution)/shard_map/scatter-add | solution.py:156
  830.3 17.9 %all-reduce = f32[1024]{0:T(1024)S(1)} all-reduce(f32[1024]{0:T(1024)S(1)} %scatter_custom_fusion.3), channel_id=2, replica_groups=mesh['grp'=4,'tile'=8] {'tile'}, use_global_device_ids=true, to_apply=%region_9.10.clone | all-reduce | flops 1024 | bytes 8192
  (670 shorter events, 465.1 us)
Async XLA Ops:
  1.5 10.9 %collective-permute-start.4 = (f32[2,1,512]{2,1,0:T(1,128)S(1)}, f32[2,1,512]{2,1,0:T(1,128)S(1)}, u32[]{:S(2)}, u32[]{:S(2)}) collective-permute-start(f32[2,1,512]{2,1,0:T(1,128)S(1)} %get-tuple-element.451), channel_id=1, source_target_pairs={{0,8},{8,16},{16,24},{1,9},{9,17},{17,25},{2,10},{10,18},{18,26},{... | collective-permute-start | bytes 12296 | tf_op jit(solution)/shard_map/ppermute | solution.py:17
  3.8 8.5 %collective-permute-start.5 = (f32[2,1,512]{2,1,0:T(1,128)S(1)}, f32[2,1,512]{2,1,0:T(1,128)S(1)}, u32[]{:S(2)}, u32[]{:S(2)}) collective-permute-start(f32[2,1,512]{2,1,0:T(1,128)S(1)} %get-tuple-element.452), channel_id=1, source_target_pairs={{8,0},{16,8},{24,16},{9,1},{17,9},{25,17},{10,2},{18,10},{26,18},{... | collective-permute-start | bytes 12296 | tf_op jit(solution)/shard_map/ppermute | solution.py:20
  5.9 12.1 %collective-permute-start = (f32[2,1,512]{2,1,0:T(1,128)S(1)}, f32[2,1,512]{2,1,0:T(1,128)S(1)}, u32[]{:S(2)}, u32[]{:S(2)}) collective-permute-start(f32[2,1,512]{2,1,0:T(1,128)S(1)} %get-tuple-element.449), channel_id=1, source_target_pairs={{0,8},{8,16},{16,24},{1,9},{9,17},{17,25},{2,10},{10,18},{18,26},{... | collective-permute-start | bytes 12296 | tf_op jit(solution)/shard_map/ppermute | solution.py:17
  11.1 6.9 collective-permute-start.1
  13.3 11.5 %collective-permute-start.6 = (f32[2,34,1]{2,1,0:T(8,128)S(1)}, f32[2,34,1]{2,1,0:T(8,128)S(1)}, u32[]{:S(2)}, u32[]{:S(2)}) collective-permute-start(f32[2,34,1]{2,1,0:T(8,128)S(1)} %get-tuple-element.387), channel_id=1, source_target_pairs={{0,1},{1,2},{2,3},{3,4},{4,5},{5,6},{6,7},{8,9},{9,10},{10,11},{11... | collective-permute-start | bytes 824 | tf_op jit(solution)/shard_map/ppermute | solution.py:17
  16.7 8.1 collective-permute-start.7
  18.9 7.0 collective-permute-start.2
  23.4 6.3 collective-permute-start.3
  36.3 6.0 collective-permute-start.9
  42.4 6.5 collective-permute-start.10
  64.4 5.9 collective-permute-start.15
  78.5 6.5 collective-permute-start.18
  100.5 5.9 collective-permute-start.23
  114.6 6.5 collective-permute-start.26
  219.5 12.5 %collective-permute-start.50 = (f32[2,34,1]{2,1,0:T(8,128)S(1)}, f32[2,34,1]{2,1,0:T(8,128)S(1)}, u32[]{:S(2)}, u32[]{:S(2)}) collective-permute-start(f32[2,34,1]{2,1,0:T(8,128)S(1)} %get-tuple-element.363), channel_id=1, source_target_pairs={{0,1},{1,2},{2,3},{3,4},{4,5},{5,6},{6,7},{8,9},{9,10},{10,11},{11... | collective-permute-start | bytes 824 | tf_op jit(solution)/shard_map/ppermute | solution.py:17
  222.3 9.7 %collective-permute-start.51 = (f32[2,34,1]{2,1,0:T(8,128)S(1)}, f32[2,34,1]{2,1,0:T(8,128)S(1)}, u32[]{:S(2)}, u32[]{:S(2)}) collective-permute-start(f32[2,34,1]{2,1,0:T(8,128)S(1)} %get-tuple-element.364), channel_id=1, source_target_pairs={{1,0},{2,1},{3,2},{4,3},{5,4},{6,5},{7,6},{9,8},{10,9},{11,10},{12... | collective-permute-start | bytes 824 | tf_op jit(solution)/shard_map/ppermute | solution.py:20
  227.1 74.6 %all-to-all-start = ((s32[32,1,32]{2,1,0:T(1,128)}), s32[32,1,32]{2,1,0:T(1,128)}, u32[]{:S(2)}, u32[]{:S(2)}) async-start(s32[32,1,32]{2,1,0:T(1,128)} %all_to_all.9), calls=%async_computation | async-start | bytes 32768 | tf_op jit(solution)/shard_map/all_to_all | solution.py:108
  240.3 60.2 %collective-permute-start.54 = (f32[2,34,1]{2,1,0:T(8,128)}, f32[2,34,1]{2,1,0:T(8,128)}, u32[]{:S(2)}, u32[]{:S(2)}) collective-permute-start(f32[2,34,1]{2,1,0:T(8,128)} %get-tuple-element.361), channel_id=1, source_target_pairs={{0,1},{1,2},{2,3},{3,4},{4,5},{5,6},{6,7},{8,9},{9,10},{10,11},{11... | collective-permute-start | bytes 824 | tf_op jit(solution)/shard_map/ppermute | solution.py:17
  244.7 55.8 %collective-permute-start.55 = (f32[2,34,1]{2,1,0:T(8,128)}, f32[2,34,1]{2,1,0:T(8,128)}, u32[]{:S(2)}, u32[]{:S(2)}) collective-permute-start(f32[2,34,1]{2,1,0:T(8,128)} %get-tuple-element.362), channel_id=1, source_target_pairs={{1,0},{2,1},{3,2},{4,3},{5,4},{6,5},{7,6},{9,8},{10,9},{11,10},{12... | collective-permute-start | bytes 824 | tf_op jit(solution)/shard_map/ppermute | solution.py:20
  301.7 126.0 %all-to-all-start.1 = ((f32[3,32,32,256]{3,2,0,1:T(8,128)}), f32[3,32,32,256]{3,2,0,1:T(8,128)}, u32[]{:S(2)}, u32[]{:S(2)}) async-start(f32[3,32,32,256]{3,2,0,1:T(8,128)} %copy.23), calls=%async_computation.1 | async-start | bytes 6291456 | tf_op jit(solution)/shard_map/all_to_all | solution.py:100
  317.3 10.7 %collective-permute-start.58 = (f32[2,34,1]{2,1,0:T(8,128)S(1)}, f32[2,34,1]{2,1,0:T(8,128)S(1)}, u32[]{:S(2)}, u32[]{:S(2)}) collective-permute-start(f32[2,34,1]{2,1,0:T(8,128)S(1)} %get-tuple-element.359), channel_id=1, source_target_pairs={{0,1},{1,2},{2,3},{3,4},{4,5},{5,6},{6,7},{8,9},{9,10},{10,11},{11... | collective-permute-start | bytes 824 | tf_op jit(solution)/shard_map/ppermute | solution.py:17
  320.6 8.7 %collective-permute-start.59 = (f32[2,34,1]{2,1,0:T(8,128)S(1)}, f32[2,34,1]{2,1,0:T(8,128)S(1)}, u32[]{:S(2)}, u32[]{:S(2)}) collective-permute-start(f32[2,34,1]{2,1,0:T(8,128)S(1)} %get-tuple-element.360), channel_id=1, source_target_pairs={{1,0},{2,1},{3,2},{4,3},{5,4},{6,5},{7,6},{9,8},{10,9},{11,10},{12... | collective-permute-start | bytes 824 | tf_op jit(solution)/shard_map/ppermute | solution.py:20
  330.6 18.6 %collective-permute-start.60 = (f32[2,1,512]{2,1,0:T(1,128)S(1)}, f32[2,1,512]{2,1,0:T(1,128)S(1)}, u32[]{:S(2)}, u32[]{:S(2)}) collective-permute-start(f32[2,1,512]{2,1,0:T(1,128)S(1)} %get-tuple-element.421), channel_id=1, source_target_pairs={{0,8},{8,16},{16,24},{1,9},{9,17},{17,25},{2,10},{10,18},{18,26},{... | collective-permute-start | bytes 12296 | tf_op jit(solution)/shard_map/ppermute | solution.py:17
  351.1 26.6 %collective-permute-start.62 = (f32[2,34,1]{2,1,0:T(8,128)S(1)}, f32[2,34,1]{2,1,0:T(8,128)S(1)}, u32[]{:S(2)}, u32[]{:S(2)}) collective-permute-start(f32[2,34,1]{2,1,0:T(8,128)S(1)} %get-tuple-element.357), channel_id=1, source_target_pairs={{0,1},{1,2},{2,3},{3,4},{4,5},{5,6},{6,7},{8,9},{9,10},{10,11},{11... | collective-permute-start | bytes 824 | tf_op jit(solution)/shard_map/ppermute | solution.py:17
  374.4 9.0 %collective-permute-start.63 = (f32[2,34,1]{2,1,0:T(8,128)S(1)}, f32[2,34,1]{2,1,0:T(8,128)S(1)}, u32[]{:S(2)}, u32[]{:S(2)}) collective-permute-start(f32[2,34,1]{2,1,0:T(8,128)S(1)} %get-tuple-element.358), channel_id=1, source_target_pairs={{1,0},{2,1},{3,2},{4,3},{5,4},{6,5},{7,6},{9,8},{10,9},{11,10},{12... | collective-permute-start | bytes 824 | tf_op jit(solution)/shard_map/ppermute | solution.py:20
  390.6 20.0 %collective-permute-start.66 = (f32[2,34,1]{2,1,0:T(8,128)S(1)}, f32[2,34,1]{2,1,0:T(8,128)S(1)}, u32[]{:S(2)}, u32[]{:S(2)}) collective-permute-start(f32[2,34,1]{2,1,0:T(8,128)S(1)} %get-tuple-element.355), channel_id=1, source_target_pairs={{0,1},{1,2},{2,3},{3,4},{4,5},{5,6},{6,7},{8,9},{9,10},{10,11},{11... | collective-permute-start | bytes 824 | tf_op jit(solution)/shard_map/ppermute | solution.py:17
  452.7 6.8 collective-permute-start.70
  471.4 6.1 collective-permute-start.74
  681.7 17.2 %collective-permute-start.124 = (f32[2,1,512]{2,1,0:T(1,128)S(1)}, f32[2,1,512]{2,1,0:T(1,128)S(1)}, u32[]{:S(2)}, u32[]{:S(2)}) collective-permute-start(f32[2,1,512]{2,1,0:T(1,128)S(1)} %get-tuple-element.389), channel_id=1, source_target_pairs={{0,8},{8,16},{16,24},{1,9},{9,17},{17,25},{2,10},{10,18},{18,26},{... | collective-permute-start | bytes 12296 | tf_op jit(solution)/shard_map/ppermute | solution.py:17
  684.5 14.4 %collective-permute-start.125 = (f32[2,1,512]{2,1,0:T(1,128)S(1)}, f32[2,1,512]{2,1,0:T(1,128)S(1)}, u32[]{:S(2)}, u32[]{:S(2)}) collective-permute-start(f32[2,1,512]{2,1,0:T(1,128)S(1)} %get-tuple-element.390), channel_id=1, source_target_pairs={{8,0},{16,8},{24,16},{9,1},{17,9},{25,17},{10,2},{18,10},{26,18},{... | collective-permute-start | bytes 12296 | tf_op jit(solution)/shard_map/ppermute | solution.py:20
  699.6 7.7 collective-permute-start.126
  703.3 6.2 collective-permute-start.127
  (170 other events, 1672.7 us)
where the time goes:
time: 864 us; the launch traced here: 849 us
  starting transfers between devices  344 us (40%)
  waiting for transfers between devices  206 us (24%)
  other arithmetic  180 us (21%)
  local copies, waits for them, and re-layouts  96 us (11%)
  blocking collectives  17.9 us (2%)
    ppermute x64, starting transfers between devices, padded_2(): lax.ppermute(lax.slice_in_dim(block, block.shape[dim] - width, None, axis...  247 us
    ppermute x64, waiting for transfers between devices, padded_2(): lax.ppermute(lax.slice_in_dim(block, 0, width, axis=dim), axis, backward)  193 us
    scatter-add x1, other arithmetic, shards(): jnp.zeros((group_width,), jnp.float32).at[local_ids].add(node_terms)  114 us
    ppermute x64, starting transfers between devices, padded_2(): lax.ppermute(lax.slice_in_dim(block, 0, width, axis=dim), axis, backward)  83.6 us
    scatter x1, local copies, waits for them, and re-layouts, shards(): jnp.zeros((3, devices * capacity, epochs), jnp.float32).at[:, row_slot]  47.5 us
    unnamed x1, blocking collectives  17.9 us
  transfers between devices with their start and end apart: 130, of which 81 were waited for; matrix products, arithmetic and copies ran while one was open for 12% of the time, Pallas kernels for 0%

commit v1 on v0

v1 whole, which is shorter than its diff:
```python
import math

import jax
import jax.numpy as jnp
from jax import lax
from jax.experimental import pallas as pl
from jax.experimental.pallas import tpu as pltpu
from jax.sharding import PartitionSpec as P

SWEEPS = 8
PICARD = 2
LANES = 128
FIELDS = 7
REACH = 32
CHUNK = 64
CHUNKS = 8
STRIP = 16
VMEM_BYTES = 60 * 1024 * 1024
NT = (((1,), (1,)), ((), ()))


def halo_pair(block, axis):
    count = lax.axis_size(axis)
    forward = [(i, i + 1) for i in range(count - 1)]
    backward = [(target, source) for source, target in forward]
    return lax.ppermute(block, axis, forward), lax.ppermute(block, axis, backward)


def thirds(values):
    first = values.astype(jnp.bfloat16)
    rest = values - first.astype(jnp.float32)
    second = rest.astype(jnp.bfloat16)
    third = (rest - second.astype(jnp.float32)).astype(jnp.bfloat16)
    return first, second, third


def one_hot(mask):
    return jnp.where(mask, 1.0, 0.0).astype(jnp.bfloat16)


def rows_kernel(groups, tiles, cap, look_ref, obs_ref, owner_ref, cell_ref, out_ref, pad_ref):
    rows = obs_ref.shape[0]
    devices = groups * tiles
    look_x, look_y, obs = look_ref[0], look_ref[1], obs_ref[...]
    lane = lax.broadcasted_iota(jnp.int32, (rows, LANES), 1)
    sums = jnp.zeros((rows, LANES), jnp.float32)
    for place, (a, b) in enumerate(
        ((look_x, look_x), (look_x, look_y), (look_y, look_y), (look_x, obs), (look_y, obs))
    ):
        sums = jnp.where(lane == place, jnp.sum(a * b, axis=1, keepdims=True), sums)
    sums = sums.T[:8]
    owner = owner_ref[...]
    cell = cell_ref[...]
    named = lax.broadcasted_iota(jnp.int32, (devices, rows), 0) == owner
    before = lax.broadcasted_iota(jnp.int32, (rows, rows), 0) < lax.broadcasted_iota(
        jnp.int32, (rows, rows), 1
    )
    ranks = jnp.dot(one_hot(named), one_hot(before), preferred_element_type=jnp.float32)
    rank = jnp.sum(jnp.where(named, ranks, 0.0), axis=0, keepdims=True)
    slot = owner * cap + rank.astype(jnp.int32)
    hit = one_hot(lax.broadcasted_iota(jnp.int32, (devices * cap, rows), 0) == slot)
    cells = jnp.concatenate(
        [
            lax.shift_right_logical(cell, 7),
            jnp.bitwise_and(cell, 127),
            jnp.zeros((6, rows), jnp.int32),
        ],
        axis=0,
    ).astype(jnp.float32)
    s0, s1, s2 = thirds(sums)
    left = jnp.concatenate(
        [s0.astype(jnp.float32), s1.astype(jnp.float32), s2.astype(jnp.float32), cells], axis=0
    ).astype(jnp.bfloat16)
    placed = lax.dot_general(left, hit, NT, preferred_element_type=jnp.float32)
    table = placed[:8] + placed[8:16] + placed[16:24]
    row = lax.broadcasted_iota(jnp.int32, table.shape, 0)
    table = jnp.where(row == 5, placed[24:25] * 128.0 + placed[25:26], table)
    edge = jnp.zeros((8, LANES), jnp.float32)
    pad_ref[:, :LANES] = edge
    pad_ref[:, LANES : LANES + devices * cap] = table
    pad_ref[:, LANES + devices * cap :] = edge
    lane8 = lax.broadcasted_iota(jnp.int32, (8, LANES), 1)
    for g in range(groups):
        for t in range(tiles):
            start = (g * tiles + t - 1) * cap + LANES
            base, off = start // LANES * LANES, start % LANES
            piece = pad_ref[:, base : base + LANES]
            if off:
                after = pad_ref[:, base + LANES : base + 2 * LANES]
                piece = jnp.where(
                    lane8 < LANES - off,
                    pltpu.roll(piece, LANES - off, 1),
                    pltpu.roll(after, LANES - off, 1),
                )
            low = cap if t == 0 else 0
            high = 2 * cap if t == tiles - 1 else 3 * cap
            piece = jnp.where((lane8 >= low) & (lane8 < high), piece, 0.0)
            for d in range(3):
                goal = g - (d - 1)
                if 0 <= goal < groups:
                    out_ref[goal * tiles + t, d * 8 : d * 8 + 8, :] = piece
    for t in range(tiles):
        out_ref[t, 0:8, :] = edge
        out_ref[(groups - 1) * tiles + t, 16:24, :] = edge


def pack_rows(groups, tiles, look, observed, row_owner, row_cell):
    rows = observed.shape[0]
    devices = groups * tiles
    cap = max(2, 2 * rows // devices)
    return pl.pallas_call(
        lambda *refs: rows_kernel(groups, tiles, cap, *refs),
        out_shape=jax.ShapeDtypeStruct((devices, 24, LANES), jnp.float32),
        scratch_shapes=[pltpu.VMEM((8, devices * cap + 2 * LANES), jnp.float32)],
        compiler_params=pltpu.CompilerParams(vmem_limit_bytes=VMEM_BYTES),
        cost_estimate=pl.CostEstimate(flops=4_000_000, bytes_accessed=4_000_000, transcendentals=0),
        name="row_sums",
    )(look, observed, row_owner.reshape(1, rows), row_cell.reshape(1, rows))


def nodes_kernel(cap, rows_x, rows_y, in_ref, mid_ref, side_ref, left_ref, right_ref):
    devices = in_ref.shape[0]
    per = LANES // cap
    slots = devices * cap
    shift = rows_y.bit_length() - 1
    lane8 = lax.broadcasted_iota(jnp.int32, (8, LANES), 1)
    for d in range(3):
        wide = rows_x if d == 1 else STRIP
        first_x = {0: rows_x - STRIP, 1: 0, 2: 0}[d]
        out_x = {0: 0, 1: STRIP, 2: STRIP + rows_x}[d]
        lists = []
        for dt in range(3):
            parts = []
            for j in range(devices // per):
                part = jnp.zeros((8, LANES), jnp.float32)
                for q in range(per):
                    source = in_ref[j * per + q, d * 8 : d * 8 + 8, :]
                    turn = (q - dt) * cap % LANES
                    moved = pltpu.roll(source, turn, 1) if turn else source
                    part = jnp.where((lane8 >= q * cap) & (lane8 < q * cap + cap), moved, part)
                parts.append(part)
            lists.append(jnp.concatenate(parts, axis=1))
        for where, out_ref, width in (((1,), mid_ref, rows_y), ((0, 2), side_ref, LANES)):
            for position, dt in enumerate(where):
                values = lists[dt]
                cell = values[5:6].astype(jnp.int32)
                cell_x = lax.shift_right_logical(cell, shift) - first_x
                cell_y = jnp.bitwise_and(cell, rows_y - 1)
                begin = position * slots
                in_x = lax.broadcasted_iota(jnp.int32, (wide, slots), 0) == cell_x
                pieces = thirds(values)
                for p in range(3):
                    piece = pieces[p].astype(jnp.float32)
                    for f in range(5):
                        at = (p * 5 + f) * wide
                        left_ref[at : at + wide, begin : begin + slots] = jnp.where(
                            in_x, piece[f : f + 1], 0.0
                        ).astype(jnp.bfloat16)
                if dt == 0:
                    cell_y = cell_y - (rows_y - LANES)
                    cell_y = jnp.where(cell_y >= LANES - STRIP, cell_y, -1)
                if dt == 2:
                    cell_y = jnp.where(cell_y < STRIP, cell_y, -1)
                right_ref[:width, begin : begin + slots] = one_hot(
                    lax.broadcasted_iota(jnp.int32, (width, slots), 0) == cell_y
                )
            total = len(where) * slots
            added = lax.dot_general(
                left_ref[: 15 * wide, :total],
                right_ref[:width, :total],
                NT,
                preferred_element_type=jnp.float32,
            )
            added = added[: 5 * wide] + added[5 * wide : 10 * wide] + added[10 * wide :]
            for f in range(5):
                out_ref[f, out_x : out_x + wide, :] = added[f * wide : (f + 1) * wide]


def add_on_nodes(arrived, cap, rows_x, rows_y):
    slots = arrived.shape[0] * cap
    high = rows_x + 2 * STRIP
    return pl.pallas_call(
        lambda *refs: nodes_kernel(cap, rows_x, rows_y, *refs),
        out_shape=(
            jax.ShapeDtypeStruct((5, high, rows_y), jnp.float32),
            jax.ShapeDtypeStruct((5, high, LANES), jnp.float32),
        ),
        scratch_shapes=[
            pltpu.VMEM((15 * rows_x, 2 * slots), jnp.bfloat16),
            pltpu.VMEM((rows_y, 2 * slots), jnp.bfloat16),
        ],
        compiler_params=pltpu.CompilerParams(vmem_limit_bytes=VMEM_BYTES),
        cost_estimate=pl.CostEstimate(flops=4_000_000, bytes_accessed=4_000_000, transcendentals=0),
        name="add_on_nodes",
    )(arrived)


def edges_kernel(low_ref, own_ref, high_ref, to_low_ref, to_high_ref):
    lane = lax.broadcasted_iota(jnp.int32, (8, LANES), 1)
    last = own_ref.shape[2] - LANES
    sources = (low_ref, own_ref, high_ref)
    for f in range(FIELDS):
        for b in range(3):
            begin = jnp.zeros((8, LANES), jnp.float32)
            end = jnp.zeros((8, LANES), jnp.float32)
            for k in range(4):
                block = 3 * k + b
                ref, at = sources[block // 4], block % 4 * 8
                mine = (lane >= 32 * k) & (lane < 32 * k + 32)
                head = ref[f, at : at + 8, :LANES]
                tail = ref[f, at : at + 8, last:]
                if k:
                    head = pltpu.roll(head, 32 * k, 1)
                if k != 3:
                    tail = pltpu.roll(tail, 32 * k + 32, 1)
                begin = jnp.where(mine, head, begin)
                end = jnp.where(mine, tail, end)
            to_low_ref[f, b * 8 : b * 8 + 8, :] = begin
            to_high_ref[f, b * 8 : b * 8 + 8, :] = end


def edges(low, own, high):
    shape = jax.ShapeDtypeStruct((FIELDS, 24, LANES), jnp.float32)
    return pl.pallas_call(
        edges_kernel,
        out_shape=(shape, shape),
        compiler_params=pltpu.CompilerParams(vmem_limit_bytes=VMEM_BYTES),
        cost_estimate=pl.CostEstimate(flops=500_000, bytes_accessed=500_000, transcendentals=0),
        name="edges",
    )(low, own, high)


def tile_rows(row, count=1):
    return slice(8 * row, 8 * (row + count))


def to_rows(pieces, left, right, store):
    lane = lax.broadcasted_iota(jnp.int32, (8, LANES), 1)
    by_32 = [left] + [pltpu.roll(p, 32, 1) for p in pieces]
    by_96 = [pltpu.roll(p, 96, 1) for p in pieces] + [right]
    for k in range(4):
        store(2 * k, jnp.where(lane < 32, by_32[k], by_32[k + 1]))
        store(2 * k + 1, jnp.where(lane < 96, by_96[k], by_96[k + 1]))


def from_rows(load):
    lane = lax.broadcasted_iota(jnp.int32, (8, LANES), 1)
    return [
        jnp.where(lane < CHUNK, pltpu.roll(load(2 * k), 96, 1), pltpu.roll(load(2 * k + 1), 32, 1))
        for k in range(4)
    ]


def stencil_rows(load_u, load_v, visc, first_row, last_row, finish):
    def lateral(row):
        u, v = load_u(row), load_v(row)
        u_next, v_next = pltpu.roll(u, LANES - 1, 1), pltpu.roll(v, LANES - 1, 1)
        return u, v, u + u_next, u_next - u, v + v_next, v_next - v

    def stresses(row, here, after):
        half, quarter = visc(row)
        x_u, y_u = after[2] - here[2], after[3] + here[3]
        x_v, y_v = after[4] - here[4], after[5] + here[5]
        both = x_u + y_v
        return half * (x_u + both), half * (y_v + both), quarter * (y_u + x_v)

    here = lateral(first_row)
    below = stresses(first_row - 1, lateral(first_row - 1), here)
    for row in range(first_row, last_row + 1):
        after = lateral(row + 1)
        above = stresses(row, here, after)
        a, c = below[0] - above[0], below[1] + above[1]
        b, e = below[2] + above[2], below[2] - above[2]
        first = pltpu.roll(a + b, 1, 1) + (a - b)
        second = pltpu.roll(c + e, 1, 1) + (e - c)
        finish(row, here[0], here[1], first, second)
        here, below = after, above


def solve_kernel(
    epochs,
    grp_count,
    tile_count,
    place_ref,
    own_ref,
    low_ref,
    high_ref,
    left_ref,
    right_ref,
    mid_ref,
    side_ref,
    ids_ref,
    out_ref,
    elem_ref,
    field,
    misfit,
    half_q,
    quarter_q,
    keep,
    prec,
    push,
    turn,
    wave_a,
    wave_b,
    seen,
    total,
    fric,
    terms,
):
    rows_x = own_ref.shape[1]
    height = rows_x + 2 * REACH
    grp, tile = place_ref[0], place_ref[1]

    sources = (low_ref, own_ref, high_ref)
    for f in range(FIELDS):
        for block in range(height // 8):
            ref, at = sources[block // 4], block % 4 * 8
            k, b = block // 3, block % 3
            left = left_ref[f, b * 8 : b * 8 + 8, :]
            right = right_ref[f, b * 8 : b * 8 + 8, :]
            if k:
                left = pltpu.roll(left, LANES - 32 * k, 1)
            if k != 3:
                right = pltpu.roll(right, 96 - 32 * k, 1)

            def store(s, value, f=f, block=block):
                field[f, pl.ds(64 * block + s, 8, stride=8), :] = value

            to_rows([ref[f, at : at + 8, LANES * j : LANES * j + LANES] for j in range(4)], left, right, store)
    for f in range(5):
        for block in range((rows_x + 2 * STRIP) // 8):
            at = block * 8
            beyond = side_ref[f, at : at + 8, :]

            def store(s, value, f=f, block=block):
                misfit[f, pl.ds(64 * block + s, 8, stride=8), :] = value

            to_rows(
                [mid_ref[f, at : at + 8, LANES * j : LANES * j + LANES] for j in range(4)],
                pltpu.roll(beyond, 32, 1),
                pltpu.roll(beyond, 96, 1),
                store,
            )

    lane = lax.broadcasted_iota(jnp.int32, (8, LANES), 1)
    chunk = lax.broadcasted_iota(jnp.int32, (8, LANES), 0)
    y = tile * (CHUNK * CHUNKS) + chunk * CHUNK + lane - 32
    in_y = (y >= 0) & (y < tile_count * (CHUNK * CHUNKS))
    in_low = in_y & jnp.broadcast_to(grp > 0, in_y.shape)
    in_high = in_y & jnp.broadcast_to(grp < grp_count - 1, in_y.shape)
    for p, (first_row, last_row) in enumerate(((2, height - 3), (2 + SWEEPS, height - 3 - SWEEPS))):

        def summed(row, p=p):
            e = field[4 + p, tile_rows(row), :]
            return e + pltpu.roll(e, LANES - 1, 1)

        before = summed(first_row - 1)
        row_sum = summed(first_row)
        quad = before + row_sum
        half_q[p, tile_rows(first_row - 1), :] = 0.125 * quad
        quarter_q[p, tile_rows(first_row - 1), :] = 0.0625 * quad
        quad_below = quad + pltpu.roll(quad, 1, 1)
        for row in range(first_row, last_row + 1):
            next_sum = summed(row + 1)
            quad = row_sum + next_sum
            half_q[p, tile_rows(row), :] = 0.125 * quad
            quarter_q[p, tile_rows(row), :] = 0.0625 * quad
            quad_above = quad + pltpu.roll(quad, 1, 1)
            fr = field[6, tile_rows(row), :]
            diagonal = (1.25 * 0.25) * (quad_below + quad_above) + fr
            inside = in_low if row < REACH else in_high if row >= REACH + rows_x else in_y
            pre = jnp.where(inside, 0.45 / diagonal, 0.0)
            prec[p, tile_rows(row), :] = pre
            keep[p, tile_rows(row), :] = 1.0 - pre * fr
            push[p, 0, tile_rows(row), :] = pre * field[2, tile_rows(row), :]
            push[p, 1, tile_rows(row), :] = pre * field[3, tile_rows(row), :]
            if p == 0:
                turn[tile_rows(row), :] = pre * (1.0 / 0.45)
            else:
                turn[tile_rows(row), :] = turn[tile_rows(row), :] * diagonal
            row_sum, quad_below = next_sum, quad_above

    def visc(p):
        return lambda row: (half_q[p, tile_rows(row), :], quarter_q[p, tile_rows(row), :])

    def forward(p, step, source, target, first_row, last_row):
        def finish(row, u, v, first, second):
            at = tile_rows(row)
            pre, rest = prec[p, at, :], keep[p, at, :]
            new_u = rest * u + push[p, 0, at, :] - pre * first
            new_v = rest * v + push[p, 1, at, :] - pre * second
            target(0, row, new_u)
            target(1, row, new_v)
            if REACH <= row < REACH + rows_x:
                here = pl.ds(8 * (row - REACH), 8)
                seen[step, 0, here, :] = u + (new_u - u) * (1.0 / 0.45)
                seen[step, 1, here, :] = v + (new_v - v) * (1.0 / 0.45)

        stencil_rows(lambda r: source(0, r), lambda r: source(1, r), visc(p), first_row, last_row, finish)

    def reader(ref):
        return lambda c, row: ref[c, tile_rows(row), :]

    def writer(ref):
        def write(c, row, value):
            ref[c, tile_rows(row), :] = value

        return write

    for c in range(2):
        wave_a[c] = field[c]
    for p in range(PICARD):
        rows = (2 + SWEEPS * p, height - 3 - SWEEPS * p)

        def pair(i, _, p=p, rows=rows):
            forward(p, SWEEPS * p + 2 * i, reader(wave_a), writer(wave_b), *rows)
            forward(p, SWEEPS * p + 2 * i + 1, reader(wave_b), writer(wave_a), *rows)
            return 0

        lax.fori_loop(0, SWEEPS // 2, pair, 0)

    first_row, last_row = 17, height - 18
    for row in range(first_row, last_row + 1):
        at, mis = tile_rows(row), tile_rows(row - (REACH - STRIP))
        u, v = wave_a[0, at, :], wave_a[1, at, :]
        cross = misfit[1, mis, :]
        scale = prec[1, at, :] * (1.0 / math.sqrt(epochs))
        wave_a[0, at, :] = scale * (misfit[0, mis, :] * u + cross * v - misfit[3, mis, :])
        wave_a[1, at, :] = scale * (cross * u + misfit[2, mis, :] * v - misfit[4, mis, :])
    total[...] = jnp.zeros_like(total)
    fric[...] = jnp.zeros_like(fric)

    def gather(step, source):
        for row in range(REACH, REACH + rows_x):
            here = tile_rows(row - REACH)
            u, v = source(0, row), source(1, row)
            total[0, here, :] = total[0, here, :] + u
            total[1, here, :] = total[1, here, :] + v
            fric[here, :] = fric[here, :] - (u * seen[step, 0, here, :] + v * seen[step, 1, here, :])

    def backward(p, step, source, target, first_row, last_row, switch=False):
        def finish(row, u, v, first, second):
            at = tile_rows(row)
            pre, rest = prec[p, at, :], keep[p, at, :]
            new_u, new_v = rest * u - pre * first, rest * v - pre * second
            if switch:
                new_u, new_v = new_u * turn[at, :], new_v * turn[at, :]
            target(0, row, new_u)
            target(1, row, new_v)
            if REACH <= row < REACH + rows_x:
                here = tile_rows(row - REACH)
                total[0, here, :] = total[0, here, :] + u
                total[1, here, :] = total[1, here, :] + v
                fric[here, :] = fric[here, :] - (u * seen[step, 0, here, :] + v * seen[step, 1, here, :])

        stencil_rows(lambda r: source(0, r), lambda r: source(1, r), visc(p), first_row, last_row, finish)

    for p in range(PICARD - 1, -1, -1):
        edge = 18 if p == PICARD - 1 else 18 + SWEEPS
        rows = (edge, height - 1 - edge)
        top = SWEEPS * (p + 1) - 1

        def pair(i, _, p=p, rows=rows, top=top):
            backward(p, top - 2 * i, reader(wave_a), writer(wave_b), *rows)
            backward(p, top - 2 * i - 1, reader(wave_b), writer(wave_a), *rows)
            return 0

        lax.fori_loop(0, SWEEPS // 2 - 1, pair, 0)
        backward(p, top - SWEEPS + 2, reader(wave_a), writer(wave_b), *rows)
        if p:
            backward(p, top - SWEEPS + 1, reader(wave_b), writer(wave_a), *rows, switch=True)
        else:
            gather(0, reader(wave_b))

    for block in range(rows_x // 8):
        at = slice(block * 8, block * 8 + 8)
        for c in range(2):
            tiles = from_rows(lambda s: total[c, pl.ds(64 * block + s, 8, stride=8), :])
            for k in range(4):
                out_ref[c, at, LANES * k : LANES * k + LANES] = tiles[k]
        tiles = from_rows(lambda s: fric[pl.ds(64 * block + s, 8, stride=8), :])
        for k in range(4):
            terms[at, LANES * k : LANES * k + LANES] = (
                tiles[k] * own_ref[6, at, LANES * k : LANES * k + LANES]
            )

    owners, elems = elem_ref.shape
    first_element = grp * (owners * elems)
    width = ids_ref.shape[1]
    owner_at = lax.broadcasted_iota(jnp.int32, (owners, width), 0)
    elem_at = lax.broadcasted_iota(jnp.int32, (elems, width), 0)
    sums = jnp.zeros((3 * owners, elems), jnp.float32)
    for row in range(rows_x):
        local = ids_ref[row : row + 1, :] - first_element
        owner = lax.shift_right_logical(local, 7)
        inside = jnp.bitwise_and(local, elems - 1)
        split = jnp.where(owner_at == owner, terms[row : row + 1, :], 0.0)
        pieces = [piece.astype(jnp.float32) for piece in thirds(split)]
        left = jnp.concatenate(pieces, axis=0).astype(jnp.bfloat16)
        sums = sums + lax.dot_general(
            left, one_hot(elem_at == inside), NT, preferred_element_type=jnp.float32
        )
    elem_ref[...] = sums[:owners] + sums[owners : 2 * owners] + sums[2 * owners :]


def solve(place, own, low, high, left, right, mid, side, ids, epochs, grp_count, tile_count):
    rows_x, rows_y = ids.shape
    height = rows_x + 2 * REACH
    elems = LANES
    tall = 8 * height
    spec = pl.BlockSpec(memory_space=pltpu.VMEM)
    f32 = jnp.float32
    return pl.pallas_call(
        lambda *refs: solve_kernel(epochs, grp_count, tile_count, *refs),
        in_specs=[pl.BlockSpec(memory_space=pltpu.SMEM)] + [spec] * 8,
        out_specs=(spec, spec),
        out_shape=(
            jax.ShapeDtypeStruct((2, rows_x, rows_y), f32),
            jax.ShapeDtypeStruct((tile_count * rows_x * rows_y // 128 // elems, elems), f32),
        ),
        scratch_shapes=[
            pltpu.VMEM((FIELDS, tall, LANES), f32),
            pltpu.VMEM((5, 8 * (rows_x + 2 * STRIP), LANES), f32),
            pltpu.VMEM((PICARD, tall, LANES), f32),
            pltpu.VMEM((PICARD, tall, LANES), f32),
            pltpu.VMEM((PICARD, tall, LANES), f32),
            pltpu.VMEM((PICARD, tall, LANES), f32),
            pltpu.VMEM((PICARD, 2, tall, LANES), f32),
            pltpu.VMEM((tall, LANES), f32),
            pltpu.VMEM((2, tall, LANES), f32),
            pltpu.VMEM((2, tall, LANES), f32),
            pltpu.VMEM((PICARD * SWEEPS, 2, 8 * rows_x, LANES), f32),
            pltpu.VMEM((2, 8 * rows_x, LANES), f32),
            pltpu.VMEM((8 * rows_x, LANES), f32),
            pltpu.VMEM((rows_x, rows_y), f32),
        ],
        compiler_params=pltpu.CompilerParams(vmem_limit_bytes=VMEM_BYTES),
        cost_estimate=pl.CostEstimate(
            flops=80_000_000, bytes_accessed=4_000_000, transcendentals=0
        ),
        name="solve",
    )(place, own, low, high, left, right, mid, side, ids)


def sum_onto_owner(terms, axis):
    count = lax.axis_size(axis)
    me = lax.axis_index(axis)
    span = 1
    terms = terms.reshape((count, 1, -1))
    while span < count:
        halves = terms.reshape((terms.shape[0] // 2, 2, -1))
        bit = me // span % 2
        mine = lax.dynamic_index_in_dim(halves, bit, 1, keepdims=False)
        other = lax.dynamic_index_in_dim(halves, 1 - bit, 1, keepdims=False)
        terms = mine + lax.ppermute(other, axis, [(i, i ^ span) for i in range(count)])
        span *= 2
    return terms.reshape(-1)


def shards(
    start_velocity,
    driving_stress,
    viscosity,
    friction,
    cell_element,
    observed,
    look,
    row_owner,
    row_cell,
):
    rows_x, rows_y = friction.shape
    row_dev, epochs = observed.shape
    groups, tiles = lax.axis_size("grp"), lax.axis_size("tile")
    devices = groups * tiles
    cap = max(2, 2 * row_dev // devices)
    own = jnp.concatenate([start_velocity, driving_stress, viscosity, friction[None]], axis=0)
    low, high = halo_pair(own, "grp")
    outgoing = pack_rows(groups, tiles, look, observed, row_owner, row_cell)
    arrived = lax.all_to_all(outgoing, ("grp", "tile"), split_axis=0, concat_axis=0, tiled=True)
    to_low, to_high = edges(low, own, high)
    count = tiles
    forward = [(i, i + 1) for i in range(count - 1)]
    backward = [(target, source) for source, target in forward]
    left = lax.ppermute(to_high, "tile", forward)
    right = lax.ppermute(to_low, "tile", backward)
    mid, side = add_on_nodes(arrived, cap, rows_x, rows_y)
    place = jnp.stack([lax.axis_index("grp"), lax.axis_index("tile")]).astype(jnp.int32)
    stress_adjoint, terms = solve(
        place, own, low, high, left, right, mid, side, cell_element, epochs, groups, tiles
    )
    return stress_adjoint, sum_onto_owner(terms, "tile")


def solution(mesh):
    return jax.shard_map(
        shards,
        mesh=mesh,
        in_specs=(
            P(None, "grp", "tile"),
            P(None, "grp", "tile"),
            P(None, "grp", "tile"),
            P("grp", "tile"),
            P("grp", "tile"),
            P(("grp", "tile"), None),
            P(None, ("grp", "tile"), None),
            P(("grp", "tile"), None),
            P(("grp", "tile")),
        ),
        out_specs=(P(None, "grp", "tile"), P(("grp", "tile"))),
        check_vma=False,
    )
```

time: 864 us -> 182 us (0.21)
  the two profiles are of different devices: /device:TPU:0 before, /device:TPU:10 now
where the time goes in v1:
time: 182 us; the launch traced here: 181 us
  Pallas kernels  139 us (76%)
  starting transfers between devices  20.2 us (11%)
  waiting for transfers between devices  17.2 us (9%)
  local copies, waits for them, and re-layouts  2.97 us (2%)
    pallas_call x1, Pallas kernels, solve(): pl.pallas_call(lambda *refs: solve_kernel(epochs, grp_count, tile_count,...  130 us
    ppermute x3, waiting for transfers between devices, sum_onto_owner(): lax.ppermute(other, axis, [(i, i ^ span) for i in range(count)])  8.61 us
    ppermute x1, waiting for transfers between devices, halo_pair(): lax.ppermute(block, axis, backward)  6.07 us
    all_to_all x1, starting transfers between devices, shards(): lax.all_to_all(outgoing, ('grp', 'tile'), split_axis=0, concat_axis=0, ti...  6.02 us
    pallas_call x1, Pallas kernels, add_on_nodes(): pl.pallas_call(lambda *refs: nodes_kernel(cap, rows_x, rows_y, *refs), ou...  4.28 us
  transfers between devices with their start and end apart: 8, of which 5 were waited for; matrix products, arithmetic and copies ran while one was open for 0% of the time, Pallas kernels for 4%

profile of v1, /device:TPU:10, one launch (start us, length us, event | category | flops | bytes accessed | tf_op | source)
XLA Modules:
  0.0 181.5 jit_solution(6456609779900377019)
XLA Ops:
  0.6 3.1 %row_sums.1 = f32[32,24,128]{2,1,0:T(8,128)} custom-call(f32[2,512,256]{2,1,0:T(8,128)} %refs_0_.1, f32[512,256]{1,0:T(8,128)} %refs_1_.1, s32[1,512]{1,0:T(1,128)} %bitcast.19, s32[1,512]{1,0:T(1,128)} %bitcast.20), custom_call_target="tpu_custom_call" | custom-call | flops 4000000 | bytes 4000000 | tf_op jit(solution)/shard_map/row_sums/pallas_call | solution.py:111
  3.8 6.0 %all-to-all-start = ((f32[32,24,128]{2,1,0:T(8,128)}), f32[32,24,128]{2,1,0:T(8,128)S(1)}, u32[]{:S(2)}, u32[]{:S(2)}) async-start(f32[32,24,128]{2,1,0:T(8,128)} %row_sums.1), calls=%async_computation | async-start | bytes 786432 | tf_op jit(solution)/shard_map/all_to_all | solution.py:579
  9.8 0.0 copy-done.4
  9.8 0.0 copy-done.5
  9.8 0.0 copy-done.6
  9.8 0.0 copy-done.9
  9.9 2.2 %collective-permute-start.1 = (f32[7,32,512]{2,1,0:T(8,128)S(1)}, f32[7,32,512]{2,1,0:T(8,128)S(1)}, u32[]{:S(2)}, u32[]{:S(2)}) collective-permute-start(f32[7,32,512]{2,1,0:T(8,128)S(1)} %pad_maximum_fusion.own_ref.refs_1_), channel_id=1, source_target_pairs={{8,0},{16,8},{24,16},{9,1},{17,9},{25,17},{10,2},{18,10},{26,18},{... | collective-permute-start | bytes 1376264 | tf_op jit(solution)/shard_map/ppermute | solution.py:26
  12.1 2.1 %collective-permute-start = (f32[7,32,512]{2,1,0:T(8,128)S(1)}, f32[7,32,512]{2,1,0:T(8,128)S(1)}, u32[]{:S(2)}, u32[]{:S(2)}) collective-permute-start(f32[7,32,512]{2,1,0:T(8,128)S(1)} %pad_maximum_fusion.own_ref.refs_1_), channel_id=1, source_target_pairs={{0,8},{8,16},{16,24},{1,9},{9,17},{17,25},{2,10},{10,18},{18,26},{... | collective-permute-start | bytes 1376264 | tf_op jit(solution)/shard_map/ppermute | solution.py:26
  14.3 6.1 %collective-permute-done.1.high_ref.refs_3_ = f32[7,32,512]{2,1,0:T(8,128)S(1)} collective-permute-done((f32[7,32,512]{2,1,0:T(8,128)S(1)}, f32[7,32,512]{2,1,0:T(8,128)S(1)}, u32[]{:S(2)}, u32[]{:S(2)}) %collective-permute-start.1) | collective-permute-done | bytes 458784 | tf_op jit(solution)/shard_map/ppermute | solution.py:26
  20.3 2.5 %collective-permute-done.low_ref.refs_2_ = f32[7,32,512]{2,1,0:T(8,128)S(1)} collective-permute-done((f32[7,32,512]{2,1,0:T(8,128)S(1)}, f32[7,32,512]{2,1,0:T(8,128)S(1)}, u32[]{:S(2)}, u32[]{:S(2)}) %collective-permute-start) | collective-permute-done | bytes 458784 | tf_op jit(solution)/shard_map/ppermute | solution.py:26
  22.8 0.0 copy-done
  22.8 0.8 copy-done.2
  23.6 2.2 %edges.1 = (f32[7,24,128]{2,1,0:T(8,128)}, f32[7,24,128]{2,1,0:T(8,128)}) custom-call(f32[7,32,512]{2,1,0:T(8,128)} %copy-done.2, f32[7,32,512]{2,1,0:T(8,128)} %copy-done, f32[7,32,512]{2,1,0:T(8,128)} %copy-done.1), custom_call_target="tpu_custom_call" | custom-call | flops 500000 | bytes 500000 | tf_op jit(solution)/shard_map/edges/pallas_call | solution.py:224
  25.8 3.6 %collective-permute-start.2 = (f32[7,24,128]{2,1,0:T(8,128)}, f32[7,24,128]{2,1,0:T(8,128)S(1)}, u32[]{:S(2)}, u32[]{:S(2)}) collective-permute-start(f32[7,24,128]{2,1,0:T(8,128)} %get-tuple-element.8), channel_id=1, source_target_pairs={{0,1},{1,2},{2,3},{3,4},{4,5},{5,6},{6,7},{8,9},{9,10},{10,11},{11... | collective-permute-start | bytes 258056 | tf_op jit(solution)/shard_map/ppermute | solution.py:584
  29.3 3.1 %collective-permute-start.3 = (f32[7,24,128]{2,1,0:T(8,128)}, f32[7,24,128]{2,1,0:T(8,128)S(1)}, u32[]{:S(2)}, u32[]{:S(2)}) collective-permute-start(f32[7,24,128]{2,1,0:T(8,128)} %get-tuple-element.9), channel_id=1, source_target_pairs={{1,0},{2,1},{3,2},{4,3},{5,4},{6,5},{7,6},{9,8},{10,9},{11,10},{12... | collective-permute-start | bytes 258056 | tf_op jit(solution)/shard_map/ppermute | solution.py:585
  32.5 0.6 pad_add_fusion.refs_0_
  33.1 0.0 all-to-all-done.refs_0_
  33.1 0.7 copy-done.3
  33.8 4.3 %add_on_nodes.1 = (f32[5,64,512]{2,1,0:T(8,128)}, f32[5,64,128]{2,1,0:T(8,128)}) custom-call(f32[32,24,128]{2,1,0:T(8,128)} %copy-done.3), custom_call_target="tpu_custom_call" | custom-call | flops 4000000 | bytes 4000000 | tf_op jit(solution)/shard_map/add_on_nodes/pallas_call | solution.py:182
  38.1 0.0 collective-permute-done.2.refs_4_
  38.1 0.0 collective-permute-done.3.refs_5_
  38.1 0.6 copy-done.7
  38.8 0.0 copy-done.8
  38.8 129.6 %solve.1 = (f32[2,32,512]{2,1,0:T(8,128)}, f32[8,128]{1,0:T(8,128)}) custom-call(s32[2]{0:T(128)} %pad_add_fusion.refs_0_, f32[7,32,512]{2,1,0:T(8,128)} %copy-done, f32[7,32,512]{2,1,0:T(8,128)} %copy-done.2, f32[7,32,512]{2,1,0:T(8,128)} %copy-done.1, f32[7,24,128]{2,1,0:T(8,128)} %copy-done.7, f32[7,24,128]{2,1,0:T(8,128)} %copy-done.8, ...), custom_call_target="tpu_custom_call" | custom-call | flops 80000000 | bytes 4000000 | tf_op jit(solution)/shard_map/solve/pallas_call | solution.py:513
  168.4 0.8 constant_dynamic-slice_fusion.4
  169.2 0.8 collective-permute-start.4
  170.0 2.8 %collective-permute-done.4 = f32[4,128]{1,0:T(4,128)S(1)} collective-permute-done((f32[4,128]{1,0:T(4,128)S(1)}, f32[4,128]{1,0:T(4,128)S(1)}, u32[]{:S(2)}, u32[]{:S(2)}) %collective-permute-start.4) | collective-permute-done | bytes 2080 | tf_op jit(solution)/shard_map/ppermute | solution.py:555
  172.8 0.1 collective-permute-start.5
  172.9 3.5 %collective-permute-done.5 = f32[2,128]{1,0:T(2,128)S(1)} collective-permute-done((f32[2,128]{1,0:T(2,128)S(1)}, f32[2,128]{1,0:T(2,128)S(1)}, u32[]{:S(2)}, u32[]{:S(2)}) %collective-permute-start.5) | collective-permute-done | bytes 1056 | tf_op jit(solution)/shard_map/ppermute | solution.py:555
  176.4 2.2 %collective-permute-start.6 = (f32[1,128]{1,0:T(1,128)S(1)}, f32[1,128]{1,0:T(1,128)S(1)}, u32[]{:S(2)}, u32[]{:S(2)}) collective-permute-start(f32[1,128]{1,0:T(1,128)S(1)} %constant_dynamic-slice_fusion), channel_id=1, source_target_pairs={{0,4},{1,5},{2,6},{3,7},{4,0},{5,1},{6,2},{7,3},{8,12},{9,13},{10,... | collective-permute-start | bytes 1544 | tf_op jit(solution)/shard_map/ppermute | solution.py:555
  178.6 2.3 %collective-permute-done.6 = f32[1,128]{1,0:T(1,128)S(1)} collective-permute-done((f32[1,128]{1,0:T(1,128)S(1)}, f32[1,128]{1,0:T(1,128)S(1)}, u32[]{:S(2)}, u32[]{:S(2)}) %collective-permute-start.6) | collective-permute-done | bytes 544 | tf_op jit(solution)/shard_map/ppermute | solution.py:555
  180.9 0.5 fusion.1
  (16 shorter events, 0.1 us)
Async XLA Ops:
  3.7 6.0 %copy-start.4 = (f32[2,32,512]{2,1,0:T(8,128)S(1)}, f32[2,32,512]{2,1,0:T(8,128)}, u32[]{:S(2)}) copy-start(f32[2,32,512]{2,1,0:T(8,128)} %param.11) | copy-start | bytes 393220
  3.7 6.1 %copy-start.5 = (f32[2,32,512]{2,1,0:T(8,128)S(1)}, f32[2,32,512]{2,1,0:T(8,128)}, u32[]{:S(2)}) copy-start(f32[2,32,512]{2,1,0:T(8,128)} %param.10) | copy-start | bytes 393220
  3.7 6.1 %copy-start.6 = (f32[2,32,512]{2,1,0:T(8,128)S(1)}, f32[2,32,512]{2,1,0:T(8,128)}, u32[]{:S(2)}) copy-start(f32[2,32,512]{2,1,0:T(8,128)} %param.9) | copy-start | bytes 393220
  3.7 6.1 %copy-start.9 = (f32[32,512]{1,0:T(8,128)S(1)}, f32[32,512]{1,0:T(8,128)}, u32[]{:S(2)}) copy-start(f32[32,512]{1,0:T(8,128)} %param.12) | copy-start | bytes 196612
  3.8 29.3 %all-to-all-start = ((f32[32,24,128]{2,1,0:T(8,128)}), f32[32,24,128]{2,1,0:T(8,128)S(1)}, u32[]{:S(2)}, u32[]{:S(2)}) async-start(f32[32,24,128]{2,1,0:T(8,128)} %row_sums.1), calls=%async_computation | async-start | bytes 786432 | tf_op jit(solution)/shard_map/all_to_all | solution.py:579
  9.9 13.0 %copy-start = (f32[7,32,512]{2,1,0:T(8,128)}, f32[7,32,512]{2,1,0:T(8,128)S(1)}, u32[]{:S(2)}) copy-start(f32[7,32,512]{2,1,0:T(8,128)S(1)} %pad_maximum_fusion.own_ref.refs_1_) | copy-start | bytes 1376260
  9.9 10.5 %collective-permute-start.1 = (f32[7,32,512]{2,1,0:T(8,128)S(1)}, f32[7,32,512]{2,1,0:T(8,128)S(1)}, u32[]{:S(2)}, u32[]{:S(2)}) collective-permute-start(f32[7,32,512]{2,1,0:T(8,128)S(1)} %pad_maximum_fusion.own_ref.refs_1_), channel_id=1, source_target_pairs={{8,0},{16,8},{24,16},{9,1},{17,9},{25,17},{10,2},{18,10},{26,18},{... | collective-permute-start | bytes 1376264 | tf_op jit(solution)/shard_map/ppermute | solution.py:26
  12.1 10.7 %collective-permute-start = (f32[7,32,512]{2,1,0:T(8,128)S(1)}, f32[7,32,512]{2,1,0:T(8,128)S(1)}, u32[]{:S(2)}, u32[]{:S(2)}) collective-permute-start(f32[7,32,512]{2,1,0:T(8,128)S(1)} %pad_maximum_fusion.own_ref.refs_1_), channel_id=1, source_target_pairs={{0,8},{8,16},{16,24},{1,9},{9,17},{17,25},{2,10},{10,18},{18,26},{... | collective-permute-start | bytes 1376264 | tf_op jit(solution)/shard_map/ppermute | solution.py:26
  20.3 2.5 %copy-start.1 = (f32[7,32,512]{2,1,0:T(8,128)}, f32[7,32,512]{2,1,0:T(8,128)S(1)}, u32[]{:S(2)}) copy-start(f32[7,32,512]{2,1,0:T(8,128)S(1)} %collective-permute-done.1.high_ref.refs_3_) | copy-start | bytes 1376260
  22.8 0.8 copy-start.2
  25.8 12.4 %collective-permute-start.2 = (f32[7,24,128]{2,1,0:T(8,128)}, f32[7,24,128]{2,1,0:T(8,128)S(1)}, u32[]{:S(2)}, u32[]{:S(2)}) collective-permute-start(f32[7,24,128]{2,1,0:T(8,128)} %get-tuple-element.8), channel_id=1, source_target_pairs={{0,1},{1,2},{2,3},{3,4},{4,5},{5,6},{6,7},{8,9},{9,10},{10,11},{11... | collective-permute-start | bytes 258056 | tf_op jit(solution)/shard_map/ppermute | solution.py:584
  29.3 8.8 %collective-permute-start.3 = (f32[7,24,128]{2,1,0:T(8,128)}, f32[7,24,128]{2,1,0:T(8,128)S(1)}, u32[]{:S(2)}, u32[]{:S(2)}) collective-permute-start(f32[7,24,128]{2,1,0:T(8,128)} %get-tuple-element.9), channel_id=1, source_target_pairs={{1,0},{2,1},{3,2},{4,3},{5,4},{6,5},{7,6},{9,8},{10,9},{11,10},{12... | collective-permute-start | bytes 258056 | tf_op jit(solution)/shard_map/ppermute | solution.py:585
  33.1 0.7 copy-start.3
  38.1 0.6 copy-start.7
  38.1 0.7 copy-start.8
  169.2 3.6 %collective-permute-start.4 = (f32[4,128]{1,0:T(4,128)S(1)}, f32[4,128]{1,0:T(4,128)S(1)}, u32[]{:S(2)}, u32[]{:S(2)}) collective-permute-start(f32[4,128]{1,0:T(4,128)S(1)} %bitcast.18), channel_id=1, source_target_pairs={{0,1},{1,0},{2,3},{3,2},{4,5},{5,4},{6,7},{7,6},{8,9},{9,8},{10,11... | collective-permute-start | bytes 6152 | tf_op jit(solution)/shard_map/ppermute | solution.py:555
  172.8 3.6 %collective-permute-start.5 = (f32[2,128]{1,0:T(2,128)S(1)}, f32[2,128]{1,0:T(2,128)S(1)}, u32[]{:S(2)}, u32[]{:S(2)}) collective-permute-start(f32[2,128]{1,0:T(2,128)S(1)} %bitcast.21), channel_id=1, source_target_pairs={{0,2},{1,3},{2,0},{3,1},{4,6},{5,7},{6,4},{7,5},{8,10},{9,11},{10,... | collective-permute-start | bytes 3080 | tf_op jit(solution)/shard_map/ppermute | solution.py:555
  176.4 4.5 %collective-permute-start.6 = (f32[1,128]{1,0:T(1,128)S(1)}, f32[1,128]{1,0:T(1,128)S(1)}, u32[]{:S(2)}, u32[]{:S(2)}) collective-permute-start(f32[1,128]{1,0:T(1,128)S(1)} %constant_dynamic-slice_fusion), channel_id=1, source_target_pairs={{0,4},{1,5},{2,6},{3,7},{4,0},{5,1},{6,2},{7,3},{8,12},{9,13},{10,... | collective-permute-start | bytes 1544 | tf_op jit(solution)/shard_map/ppermute | solution.py:555

commit v2 on v1

--- a/solution.py
+++ b/solution.py
@@ -14,6 +14,7 @@
 REACH = 32
 CHUNK = 64
 CHUNKS = 8
+DELAY = 8
 STRIP = 16
 VMEM_BYTES = 60 * 1024 * 1024
 NT = (((1,), (1,)), ((), ()))
@@ -252,29 +253,49 @@
 
 
 def stencil_rows(load_u, load_v, visc, first_row, last_row, finish):
+    ahead = {}
+    waiting = []
+
+    def issue(row):
+        if row <= last_row + 1:
+            ahead[row] = (
+                pltpu.roll(load_u(row), LANES - 1, 1),
+                pltpu.roll(load_v(row), LANES - 1, 1),
+            )
+
     def lateral(row):
         u, v = load_u(row), load_v(row)
-        u_next, v_next = pltpu.roll(u, LANES - 1, 1), pltpu.roll(v, LANES - 1, 1)
-        return u, v, u + u_next, u_next - u, v + v_next, v_next - v
+        u_next, v_next = ahead.pop(row)
+        return u + u_next, u_next - u, v + v_next, v_next - v
 
     def stresses(row, here, after):
         half, quarter = visc(row)
-        x_u, y_u = after[2] - here[2], after[3] + here[3]
-        x_v, y_v = after[4] - here[4], after[5] + here[5]
+        x_u, y_u = after[0] - here[0], after[1] + here[1]
+        x_v, y_v = after[2] - here[2], after[3] + here[3]
         both = x_u + y_v
         return half * (x_u + both), half * (y_v + both), quarter * (y_u + x_v)
 
+    def flush():
+        row, turned_first, still_first, turned_second, still_second = waiting.pop(0)
+        finish(row, load_u(row), load_v(row), turned_first + still_first, turned_second + still_second)
+
+    for row in range(first_row - 1, first_row + 1 + DELAY):
+        issue(row)
+    before = lateral(first_row - 1)
     here = lateral(first_row)
-    below = stresses(first_row - 1, lateral(first_row - 1), here)
+    below = stresses(first_row - 1, before, here)
     for row in range(first_row, last_row + 1):
+        issue(row + 1 + DELAY)
         after = lateral(row + 1)
         above = stresses(row, here, after)
         a, c = below[0] - above[0], below[1] + above[1]
         b, e = below[2] + above[2], below[2] - above[2]
-        first = pltpu.roll(a + b, 1, 1) + (a - b)
-        second = pltpu.roll(c + e, 1, 1) + (e - c)
-        finish(row, here[0], here[1], first, second)
+        waiting.append((row, pltpu.roll(a + b, 1, 1), a - b, pltpu.roll(c + e, 1, 1), e - c))
+        if len(waiting) > DELAY:
+            flush()
         here, below = after, above
+    while waiting:
+        flush()
 
 
 def solve_kernel(

time: 182 us -> 77 us (0.42)
  Pallas kernels: 139 us -> 34.3 us
    pallas_call x1, Pallas kernels: 130 us -> 24.8 us  [solve(): pl.pallas_call(lambda *refs: solve_kernel(epochs, grp_count, tile_count,...]
  transfers between devices with their start and end apart: 8 -> 8, of which waited for: 5 -> 5; matrix products, arithmetic and copies ran while one was open for 0% -> 1% of each run, Pallas kernels for 4% -> 8%
where the time goes in v2:
time: 77 us; the launch traced here: 76.6 us
  Pallas kernels  34.3 us (45%)
  starting transfers between devices  20.2 us (26%)
  waiting for transfers between devices  17.2 us (22%)
  local copies, waits for them, and re-layouts  2.97 us (4%)
  other arithmetic  1.15 us (1%)
  between operations  0.82 us (1%)
    pallas_call x1, Pallas kernels, solve(): pl.pallas_call(lambda *refs: solve_kernel(epochs, grp_count, tile_count,...  24.8 us
    ppermute x3, waiting for transfers between devices, sum_onto_owner(): lax.ppermute(other, axis, [(i, i ^ span) for i in range(count)])  8.62 us
    ppermute x1, waiting for transfers between devices, halo_pair(): lax.ppermute(block, axis, backward)  6.07 us
    all_to_all x1, starting transfers between devices, shards(): lax.all_to_all(outgoing, ('grp', 'tile'), split_axis=0, concat_axis=0, ti...  6.02 us
    pallas_call x1, Pallas kernels, add_on_nodes(): pl.pallas_call(lambda *refs: nodes_kernel(cap, rows_x, rows_y, *refs), ou...  4.28 us
    ppermute x1, starting transfers between devices, shards(): left = lax.ppermute(to_high, 'tile', forward)  3.59 us
    ppermute x1, starting transfers between devices, shards(): right = lax.ppermute(to_low, 'tile', backward)  3.14 us
    pallas_call x1, Pallas kernels, pack_rows(): pl.pallas_call(lambda *refs: rows_kernel(groups, tiles, cap, *refs), out_...  3.11 us
  transfers between devices with their start and end apart: 8, of which 5 were waited for; matrix products, arithmetic and copies ran while one was open for 1% of the time, Pallas kernels for 8%

profile of v2, /device:TPU:10, one launch (start us, length us, event | category | flops | bytes accessed | tf_op | source)
XLA Modules:
  0.0 76.6 jit_solution(9872507425619464931)
XLA Ops:
  0.6 3.1 %row_sums.1 = f32[32,24,128]{2,1,0:T(8,128)} custom-call(f32[2,512,256]{2,1,0:T(8,128)} %refs_0_.1, f32[512,256]{1,0:T(8,128)} %refs_1_.1, s32[1,512]{1,0:T(1,128)} %bitcast.19, s32[1,512]{1,0:T(1,128)} %bitcast.20), custom_call_target="tpu_custom_call" | custom-call | flops 4000000 | bytes 4000000 | tf_op jit(solution)/shard_map/row_sums/pallas_call | solution.py:112
  3.8 6.0 %all-to-all-start = ((f32[32,24,128]{2,1,0:T(8,128)}), f32[32,24,128]{2,1,0:T(8,128)S(1)}, u32[]{:S(2)}, u32[]{:S(2)}) async-start(f32[32,24,128]{2,1,0:T(8,128)} %row_sums.1), calls=%async_computation | async-start | bytes 786432 | tf_op jit(solution)/shard_map/all_to_all | solution.py:600
  9.8 0.0 copy-done.4
  9.8 0.0 copy-done.5
  9.8 0.0 copy-done.6
  9.8 0.0 copy-done.9
  9.9 0.0 copy-start
  9.9 2.2 %collective-permute-start.1 = (f32[7,32,512]{2,1,0:T(8,128)S(1)}, f32[7,32,512]{2,1,0:T(8,128)S(1)}, u32[]{:S(2)}, u32[]{:S(2)}) collective-permute-start(f32[7,32,512]{2,1,0:T(8,128)S(1)} %pad_maximum_fusion.own_ref.refs_1_), channel_id=1, source_target_pairs={{8,0},{16,8},{24,16},{9,1},{17,9},{25,17},{10,2},{18,10},{26,18},{... | collective-permute-start | bytes 1376264 | tf_op jit(solution)/shard_map/ppermute | solution.py:27
  12.1 2.1 %collective-permute-start = (f32[7,32,512]{2,1,0:T(8,128)S(1)}, f32[7,32,512]{2,1,0:T(8,128)S(1)}, u32[]{:S(2)}, u32[]{:S(2)}) collective-permute-start(f32[7,32,512]{2,1,0:T(8,128)S(1)} %pad_maximum_fusion.own_ref.refs_1_), channel_id=1, source_target_pairs={{0,8},{8,16},{16,24},{1,9},{9,17},{17,25},{2,10},{10,18},{18,26},{... | collective-permute-start | bytes 1376264 | tf_op jit(solution)/shard_map/ppermute | solution.py:27
  14.3 6.1 %collective-permute-done.1.high_ref.refs_3_ = f32[7,32,512]{2,1,0:T(8,128)S(1)} collective-permute-done((f32[7,32,512]{2,1,0:T(8,128)S(1)}, f32[7,32,512]{2,1,0:T(8,128)S(1)}, u32[]{:S(2)}, u32[]{:S(2)}) %collective-permute-start.1) | collective-permute-done | bytes 458784 | tf_op jit(solution)/shard_map/ppermute | solution.py:27
  20.3 2.5 %collective-permute-done.low_ref.refs_2_ = f32[7,32,512]{2,1,0:T(8,128)S(1)} collective-permute-done((f32[7,32,512]{2,1,0:T(8,128)S(1)}, f32[7,32,512]{2,1,0:T(8,128)S(1)}, u32[]{:S(2)}, u32[]{:S(2)}) %collective-permute-start) | collective-permute-done | bytes 458784 | tf_op jit(solution)/shard_map/ppermute | solution.py:27
  22.8 0.8 copy-done.2
  23.6 2.2 %edges.1 = (f32[7,24,128]{2,1,0:T(8,128)}, f32[7,24,128]{2,1,0:T(8,128)}) custom-call(f32[7,32,512]{2,1,0:T(8,128)} %copy-done.2, f32[7,32,512]{2,1,0:T(8,128)} %copy-done, f32[7,32,512]{2,1,0:T(8,128)} %copy-done.1), custom_call_target="tpu_custom_call" | custom-call | flops 500000 | bytes 500000 | tf_op jit(solution)/shard_map/edges/pallas_call | solution.py:225
  25.8 3.6 %collective-permute-start.2 = (f32[7,24,128]{2,1,0:T(8,128)}, f32[7,24,128]{2,1,0:T(8,128)S(1)}, u32[]{:S(2)}, u32[]{:S(2)}) collective-permute-start(f32[7,24,128]{2,1,0:T(8,128)} %get-tuple-element.8), channel_id=1, source_target_pairs={{0,1},{1,2},{2,3},{3,4},{4,5},{5,6},{6,7},{8,9},{9,10},{10,11},{11... | collective-permute-start | bytes 258056 | tf_op jit(solution)/shard_map/ppermute | solution.py:605
  29.3 3.1 %collective-permute-start.3 = (f32[7,24,128]{2,1,0:T(8,128)}, f32[7,24,128]{2,1,0:T(8,128)S(1)}, u32[]{:S(2)}, u32[]{:S(2)}) collective-permute-start(f32[7,24,128]{2,1,0:T(8,128)} %get-tuple-element.9), channel_id=1, source_target_pairs={{1,0},{2,1},{3,2},{4,3},{5,4},{6,5},{7,6},{9,8},{10,9},{11,10},{12... | collective-permute-start | bytes 258056 | tf_op jit(solution)/shard_map/ppermute | solution.py:606
  32.5 0.6 pad_add_fusion.refs_0_
  33.1 0.0 all-to-all-done.refs_0_
  33.1 0.7 copy-done.3
  33.8 4.3 %add_on_nodes.1 = (f32[5,64,512]{2,1,0:T(8,128)}, f32[5,64,128]{2,1,0:T(8,128)}) custom-call(f32[32,24,128]{2,1,0:T(8,128)} %copy-done.3), custom_call_target="tpu_custom_call" | custom-call | flops 4000000 | bytes 4000000 | tf_op jit(solution)/shard_map/add_on_nodes/pallas_call | solution.py:183
  38.1 0.0 collective-permute-done.2.refs_4_
  38.1 0.0 collective-permute-done.3.refs_5_
  38.1 0.6 copy-done.7
  38.8 0.0 copy-done.8
  38.8 24.8 %solve.1 = (f32[2,32,512]{2,1,0:T(8,128)}, f32[8,128]{1,0:T(8,128)}) custom-call(s32[2]{0:T(128)} %pad_add_fusion.refs_0_, f32[7,32,512]{2,1,0:T(8,128)} %copy-done, f32[7,32,512]{2,1,0:T(8,128)} %copy-done.2, f32[7,32,512]{2,1,0:T(8,128)} %copy-done.1, f32[7,24,128]{2,1,0:T(8,128)} %copy-done.7, f32[7,24,128]{2,1,0:T(8,128)} %copy-done.8, ...), custom_call_target="tpu_custom_call" | custom-call | flops 80000000 | bytes 4000000 | tf_op jit(solution)/shard_map/solve/pallas_call | solution.py:534
  63.6 0.8 constant_dynamic-slice_fusion.4
  64.3 0.8 %collective-permute-start.4 = (f32[4,128]{1,0:T(4,128)S(1)}, f32[4,128]{1,0:T(4,128)S(1)}, u32[]{:S(2)}, u32[]{:S(2)}) collective-permute-start(f32[4,128]{1,0:T(4,128)S(1)} %bitcast.18), channel_id=1, source_target_pairs={{0,1},{1,0},{2,3},{3,2},{4,5},{5,4},{6,7},{7,6},{8,9},{9,8},{10,11... | collective-permute-start | bytes 6152 | tf_op jit(solution)/shard_map/ppermute | solution.py:576
  65.1 2.8 %collective-permute-done.4 = f32[4,128]{1,0:T(4,128)S(1)} collective-permute-done((f32[4,128]{1,0:T(4,128)S(1)}, f32[4,128]{1,0:T(4,128)S(1)}, u32[]{:S(2)}, u32[]{:S(2)}) %collective-permute-start.4) | collective-permute-done | bytes 2080 | tf_op jit(solution)/shard_map/ppermute | solution.py:576
  67.9 0.1 collective-permute-start.5
  68.0 3.5 %collective-permute-done.5 = f32[2,128]{1,0:T(2,128)S(1)} collective-permute-done((f32[2,128]{1,0:T(2,128)S(1)}, f32[2,128]{1,0:T(2,128)S(1)}, u32[]{:S(2)}, u32[]{:S(2)}) %collective-permute-start.5) | collective-permute-done | bytes 1056 | tf_op jit(solution)/shard_map/ppermute | solution.py:576
  71.6 2.2 %collective-permute-start.6 = (f32[1,128]{1,0:T(1,128)S(1)}, f32[1,128]{1,0:T(1,128)S(1)}, u32[]{:S(2)}, u32[]{:S(2)}) collective-permute-start(f32[1,128]{1,0:T(1,128)S(1)} %constant_dynamic-slice_fusion), channel_id=1, source_target_pairs={{0,4},{1,5},{2,6},{3,7},{4,0},{5,1},{6,2},{7,3},{8,12},{9,13},{10,... | collective-permute-start | bytes 1544 | tf_op jit(solution)/shard_map/ppermute | solution.py:576
  73.8 2.3 %collective-permute-done.6 = f32[1,128]{1,0:T(1,128)S(1)} collective-permute-done((f32[1,128]{1,0:T(1,128)S(1)}, f32[1,128]{1,0:T(1,128)S(1)}, u32[]{:S(2)}, u32[]{:S(2)}) %collective-permute-start.6) | collective-permute-done | bytes 544 | tf_op jit(solution)/shard_map/ppermute | solution.py:576
  76.1 0.5 fusion.1
  (16 shorter events, 0.1 us)
Async XLA Ops:
  3.7 6.0 %copy-start.4 = (f32[2,32,512]{2,1,0:T(8,128)S(1)}, f32[2,32,512]{2,1,0:T(8,128)}, u32[]{:S(2)}) copy-start(f32[2,32,512]{2,1,0:T(8,128)} %param.11) | copy-start | bytes 393220
  3.7 6.1 %copy-start.5 = (f32[2,32,512]{2,1,0:T(8,128)S(1)}, f32[2,32,512]{2,1,0:T(8,128)}, u32[]{:S(2)}) copy-start(f32[2,32,512]{2,1,0:T(8,128)} %param.10) | copy-start | bytes 393220
  3.7 6.1 %copy-start.6 = (f32[2,32,512]{2,1,0:T(8,128)S(1)}, f32[2,32,512]{2,1,0:T(8,128)}, u32[]{:S(2)}) copy-start(f32[2,32,512]{2,1,0:T(8,128)} %param.9) | copy-start | bytes 393220
  3.7 6.1 %copy-start.9 = (f32[32,512]{1,0:T(8,128)S(1)}, f32[32,512]{1,0:T(8,128)}, u32[]{:S(2)}) copy-start(f32[32,512]{1,0:T(8,128)} %param.12) | copy-start | bytes 196612
  3.8 29.3 %all-to-all-start = ((f32[32,24,128]{2,1,0:T(8,128)}), f32[32,24,128]{2,1,0:T(8,128)S(1)}, u32[]{:S(2)}, u32[]{:S(2)}) async-start(f32[32,24,128]{2,1,0:T(8,128)} %row_sums.1), calls=%async_computation | async-start | bytes 786432 | tf_op jit(solution)/shard_map/all_to_all | solution.py:600
  9.9 13.0 %copy-start = (f32[7,32,512]{2,1,0:T(8,128)}, f32[7,32,512]{2,1,0:T(8,128)S(1)}, u32[]{:S(2)}) copy-start(f32[7,32,512]{2,1,0:T(8,128)S(1)} %pad_maximum_fusion.own_ref.refs_1_) | copy-start | bytes 1376260
  9.9 10.5 %collective-permute-start.1 = (f32[7,32,512]{2,1,0:T(8,128)S(1)}, f32[7,32,512]{2,1,0:T(8,128)S(1)}, u32[]{:S(2)}, u32[]{:S(2)}) collective-permute-start(f32[7,32,512]{2,1,0:T(8,128)S(1)} %pad_maximum_fusion.own_ref.refs_1_), channel_id=1, source_target_pairs={{8,0},{16,8},{24,16},{9,1},{17,9},{25,17},{10,2},{18,10},{26,18},{... | collective-permute-start | bytes 1376264 | tf_op jit(solution)/shard_map/ppermute | solution.py:27
  12.1 10.7 %collective-permute-start = (f32[7,32,512]{2,1,0:T(8,128)S(1)}, f32[7,32,512]{2,1,0:T(8,128)S(1)}, u32[]{:S(2)}, u32[]{:S(2)}) collective-permute-start(f32[7,32,512]{2,1,0:T(8,128)S(1)} %pad_maximum_fusion.own_ref.refs_1_), channel_id=1, source_target_pairs={{0,8},{8,16},{16,24},{1,9},{9,17},{17,25},{2,10},{10,18},{18,26},{... | collective-permute-start | bytes 1376264 | tf_op jit(solution)/shard_map/ppermute | solution.py:27
  20.3 2.5 %copy-start.1 = (f32[7,32,512]{2,1,0:T(8,128)}, f32[7,32,512]{2,1,0:T(8,128)S(1)}, u32[]{:S(2)}) copy-start(f32[7,32,512]{2,1,0:T(8,128)S(1)} %collective-permute-done.1.high_ref.refs_3_) | copy-start | bytes 1376260
  22.8 0.8 %copy-start.2 = (f32[7,32,512]{2,1,0:T(8,128)}, f32[7,32,512]{2,1,0:T(8,128)S(1)}, u32[]{:S(2)}) copy-start(f32[7,32,512]{2,1,0:T(8,128)S(1)} %collective-permute-done.low_ref.refs_2_) | copy-start | bytes 1376260
  25.8 12.4 %collective-permute-start.2 = (f32[7,24,128]{2,1,0:T(8,128)}, f32[7,24,128]{2,1,0:T(8,128)S(1)}, u32[]{:S(2)}, u32[]{:S(2)}) collective-permute-start(f32[7,24,128]{2,1,0:T(8,128)} %get-tuple-element.8), channel_id=1, source_target_pairs={{0,1},{1,2},{2,3},{3,4},{4,5},{5,6},{6,7},{8,9},{9,10},{10,11},{11... | collective-permute-start | bytes 258056 | tf_op jit(solution)/shard_map/ppermute | solution.py:605
  29.3 8.8 %collective-permute-start.3 = (f32[7,24,128]{2,1,0:T(8,128)}, f32[7,24,128]{2,1,0:T(8,128)S(1)}, u32[]{:S(2)}, u32[]{:S(2)}) collective-permute-start(f32[7,24,128]{2,1,0:T(8,128)} %get-tuple-element.9), channel_id=1, source_target_pairs={{1,0},{2,1},{3,2},{4,3},{5,4},{6,5},{7,6},{9,8},{10,9},{11,10},{12... | collective-permute-start | bytes 258056 | tf_op jit(solution)/shard_map/ppermute | solution.py:606
  33.1 0.7 copy-start.3
  38.1 0.6 copy-start.7
  38.1 0.7 copy-start.8
  64.3 3.6 %collective-permute-start.4 = (f32[4,128]{1,0:T(4,128)S(1)}, f32[4,128]{1,0:T(4,128)S(1)}, u32[]{:S(2)}, u32[]{:S(2)}) collective-permute-start(f32[4,128]{1,0:T(4,128)S(1)} %bitcast.18), channel_id=1, source_target_pairs={{0,1},{1,0},{2,3},{3,2},{4,5},{5,4},{6,7},{7,6},{8,9},{9,8},{10,11... | collective-permute-start | bytes 6152 | tf_op jit(solution)/shard_map/ppermute | solution.py:576
  67.9 3.6 %collective-permute-start.5 = (f32[2,128]{1,0:T(2,128)S(1)}, f32[2,128]{1,0:T(2,128)S(1)}, u32[]{:S(2)}, u32[]{:S(2)}) collective-permute-start(f32[2,128]{1,0:T(2,128)S(1)} %bitcast.21), channel_id=1, source_target_pairs={{0,2},{1,3},{2,0},{3,1},{4,6},{5,7},{6,4},{7,5},{8,10},{9,11},{10,... | collective-permute-start | bytes 3080 | tf_op jit(solution)/shard_map/ppermute | solution.py:576
  71.6 4.5 %collective-permute-start.6 = (f32[1,128]{1,0:T(1,128)S(1)}, f32[1,128]{1,0:T(1,128)S(1)}, u32[]{:S(2)}, u32[]{:S(2)}) collective-permute-start(f32[1,128]{1,0:T(1,128)S(1)} %constant_dynamic-slice_fusion), channel_id=1, source_target_pairs={{0,4},{1,5},{2,6},{3,7},{4,0},{5,1},{6,2},{7,3},{8,12},{9,13},{10,... | collective-permute-start | bytes 1544 | tf_op jit(solution)/shard_map/ppermute | solution.py:576

commit v3 on v2

--- a/solution.py
+++ b/solution.py
@@ -14,9 +14,9 @@
 REACH = 32
 CHUNK = 64
 CHUNKS = 8
-DELAY = 8
+DELAY = 14
 STRIP = 16
-VMEM_BYTES = 60 * 1024 * 1024
+MIB = 1024 * 1024
 NT = (((1,), (1,)), ((), ()))
 
 
@@ -113,8 +113,8 @@
         lambda *refs: rows_kernel(groups, tiles, cap, *refs),
         out_shape=jax.ShapeDtypeStruct((devices, 24, LANES), jnp.float32),
         scratch_shapes=[pltpu.VMEM((8, devices * cap + 2 * LANES), jnp.float32)],
-        compiler_params=pltpu.CompilerParams(vmem_limit_bytes=VMEM_BYTES),
-        cost_estimate=pl.CostEstimate(flops=4_000_000, bytes_accessed=4_000_000, transcendentals=0),
+        compiler_params=pltpu.CompilerParams(vmem_limit_bytes=12 * MIB),
+        cost_estimate=pl.CostEstimate(flops=4_000_000, bytes_accessed=80_000_000, transcendentals=0),
         name="row_sums",
     )(look, observed, row_owner.reshape(1, rows), row_cell.reshape(1, rows))
 
@@ -190,26 +190,24 @@
             pltpu.VMEM((15 * rows_x, 2 * slots), jnp.bfloat16),
             pltpu.VMEM((rows_y, 2 * slots), jnp.bfloat16),
         ],
-        compiler_params=pltpu.CompilerParams(vmem_limit_bytes=VMEM_BYTES),
+        compiler_params=pltpu.CompilerParams(vmem_limit_bytes=16 * MIB),
         cost_estimate=pl.CostEstimate(flops=4_000_000, bytes_accessed=4_000_000, transcendentals=0),
         name="add_on_nodes",
     )(arrived)
 
 
-def edges_kernel(low_ref, own_ref, high_ref, to_low_ref, to_high_ref):
+def edges_kernel(*refs):
+    heads, tails, (to_low_ref, to_high_ref) = refs[:3], refs[3:6], refs[6:]
     lane = lax.broadcasted_iota(jnp.int32, (8, LANES), 1)
-    last = own_ref.shape[2] - LANES
-    sources = (low_ref, own_ref, high_ref)
     for f in range(FIELDS):
         for b in range(3):
             begin = jnp.zeros((8, LANES), jnp.float32)
             end = jnp.zeros((8, LANES), jnp.float32)
             for k in range(4):
                 block = 3 * k + b
-                ref, at = sources[block // 4], block % 4 * 8
+                at = block % 4 * 8
                 mine = (lane >= 32 * k) & (lane < 32 * k + 32)
-                head = ref[f, at : at + 8, :LANES]
-                tail = ref[f, at : at + 8, last:]
+                head, tail = heads[block // 4][f, at : at + 8, :], tails[block // 4][f, at : at + 8, :]
                 if k:
                     head = pltpu.roll(head, 32 * k, 1)
                 if k != 3:
@@ -222,13 +220,21 @@
 
 def edges(low, own, high):
     shape = jax.ShapeDtypeStruct((FIELDS, 24, LANES), jnp.float32)
+    part = (FIELDS, own.shape[1], LANES)
+    last = own.shape[2] // LANES - 1
+    head = pl.BlockSpec(part, lambda i: (0, 0, 0))
+    tail = pl.BlockSpec(part, lambda i: (0, 0, last))
+    whole = pl.BlockSpec(shape.shape, lambda i: (0, 0, 0))
     return pl.pallas_call(
         edges_kernel,
+        grid=(1,),
+        in_specs=[head] * 3 + [tail] * 3,
+        out_specs=(whole, whole),
         out_shape=(shape, shape),
-        compiler_params=pltpu.CompilerParams(vmem_limit_bytes=VMEM_BYTES),
-        cost_estimate=pl.CostEstimate(flops=500_000, bytes_accessed=500_000, transcendentals=0),
+        compiler_params=pltpu.CompilerParams(vmem_limit_bytes=4 * MIB),
+        cost_estimate=pl.CostEstimate(flops=100_000_000_000, bytes_accessed=500_000, transcendentals=0),
         name="edges",
-    )(low, own, high)
+    )(low, own, high, low, own, high)
 
 
 def tile_rows(row, count=1):
@@ -555,7 +561,7 @@
             pltpu.VMEM((8 * rows_x, LANES), f32),
             pltpu.VMEM((rows_x, rows_y), f32),
         ],
-        compiler_params=pltpu.CompilerParams(vmem_limit_bytes=VMEM_BYTES),
+        compiler_params=pltpu.CompilerParams(vmem_limit_bytes=28 * MIB),
         cost_estimate=pl.CostEstimate(
             flops=80_000_000, bytes_accessed=4_000_000, transcendentals=0
         ),

time: 77 us -> 63.8 us (0.83)
  the two profiles are of different devices: /device:TPU:10 before, /device:TPU:0 now
where the time goes in v3:
time: 63.8 us; the launch traced here: 63.5 us
  Pallas kernels  23 us (36%)
  starting transfers between devices  18.9 us (30%)
  waiting for transfers between devices  17.7 us (28%)
  other arithmetic  1.75 us (3%)
  local copies, waits for them, and re-layouts  1.26 us (2%)
  between operations  0.84 us (1%)
    pallas_call x1, Pallas kernels, solve(): pl.pallas_call(lambda *refs: solve_kernel(epochs, grp_count, tile_count,...  18.7 us
    ppermute x3, waiting for transfers between devices, sum_onto_owner(): lax.ppermute(other, axis, [(i, i ^ span) for i in range(count)])  9.51 us
    all_to_all x1, waiting for transfers between devices, shards(): lax.all_to_all(outgoing, ('grp', 'tile'), split_axis=0, concat_axis=0, ti...  8.23 us
    all_to_all x1, starting transfers between devices, shards(): lax.all_to_all(outgoing, ('grp', 'tile'), split_axis=0, concat_axis=0, ti...  7.3 us
    ppermute x1, starting transfers between devices, shards(): left = lax.ppermute(to_high, 'tile', forward)  3.68 us
    ppermute x1, starting transfers between devices, halo_pair(): lax.ppermute(block, axis, forward)  3.06 us
    pallas_call x1, Pallas kernels, add_on_nodes(): pl.pallas_call(lambda *refs: nodes_kernel(cap, rows_x, rows_y, *refs), ou...  2.36 us
    ppermute x3, starting transfers between devices, sum_onto_owner(): lax.ppermute(other, axis, [(i, i ^ span) for i in range(count)])  2.26 us
  transfers between devices with their start and end apart: 8, of which 4 were waited for; matrix products, arithmetic and copies ran while one was open for 0% of the time, Pallas kernels for 7%

profile of v3, /device:TPU:0, one launch (start us, length us, event | category | flops | bytes accessed | tf_op | source)
XLA Modules:
  0.0 63.5 jit_solution(17061782109777021985)
XLA Ops:
  0.6 0.0 copy-start.1
  0.6 0.0 copy-start.4
  0.7 1.1 %pad_maximum_fusion.refs_1_.refs_4_ = f32[7,32,512]{2,1,0:T(8,128)S(1)} fusion(f32[1,32,512]{2,1,0:T(8,128)} %bitcast.16, f32[2,32,512]{2,1,0:T(8,128)} %param.11, f32[2,32,512]{2,1,0:T(8,128)} %param.10, f32[2,32,512]{2,1,0:T(8,128)} %param.9), kind=kLoop, calls=%fused_computation | loop fusion | flops 344064 | bytes 917504 | tf_op jit(solution)/shard_map/concatenate | solution.py:603
  1.8 0.0 copy-start.3
  1.8 1.3 %collective-permute-start.1 = (f32[7,32,512]{2,1,0:T(8,128)S(1)}, f32[7,32,512]{2,1,0:T(8,128)S(1)}, u32[]{:S(2)}, u32[]{:S(2)}) collective-permute-start(f32[7,32,512]{2,1,0:T(8,128)S(1)} %pad_maximum_fusion.refs_1_.refs_4_), channel_id=1, source_target_pairs={{8,0},{16,8},{24,16},{9,1},{17,9},{25,17},{10,2},{18,10},{26,18},{... | collective-permute-start | bytes 1376264 | tf_op jit(solution)/shard_map/ppermute | solution.py:27
  3.1 3.1 %collective-permute-start = (f32[7,32,512]{2,1,0:T(8,128)S(1)}, f32[7,32,512]{2,1,0:T(8,128)S(1)}, u32[]{:S(2)}, u32[]{:S(2)}) collective-permute-start(f32[7,32,512]{2,1,0:T(8,128)S(1)} %pad_maximum_fusion.refs_1_.refs_4_), channel_id=1, source_target_pairs={{0,8},{8,16},{16,24},{1,9},{9,17},{17,25},{2,10},{10,18},{18,26},{... | collective-permute-start | bytes 1376264 | tf_op jit(solution)/shard_map/ppermute | solution.py:27
  6.2 0.0 copy-done.1
  6.2 0.0 copy-done.4
  6.2 0.0 copy-done.3
  6.2 0.0 copy-start
  6.2 1.2 %copy-done = f32[2,512,256]{2,1,0:T(8,128)S(1)} copy-done((f32[2,512,256]{2,1,0:T(8,128)S(1)}, f32[2,512,256]{2,1,0:T(8,128)}, u32[]{:S(2)}) %copy-start) | copy-done | bytes 1048600
  7.4 1.7 %row_sums.1 = f32[32,24,128]{2,1,0:T(8,128)} custom-call(f32[2,512,256]{2,1,0:T(8,128)S(1)} %copy-done, f32[512,256]{1,0:T(8,128)S(1)} %copy-done.1, s32[1,512]{1,0:T(1,128)S(1)} %bitcast.14, s32[1,512]{1,0:T(1,128)S(1)} %bitcast.15), custom_call_target="tpu_custom_call" | custom-call | flops 4000000 | bytes 80000000 | tf_op jit(solution)/shard_map/row_sums/pallas_call | solution.py:112
  9.2 7.3 %all-to-all-start = ((f32[32,24,128]{2,1,0:T(8,128)}), f32[32,24,128]{2,1,0:T(8,128)S(1)}, u32[]{:S(2)}, u32[]{:S(2)}) async-start(f32[32,24,128]{2,1,0:T(8,128)} %row_sums.1), calls=%async_computation | async-start | bytes 786432 | tf_op jit(solution)/shard_map/all_to_all | solution.py:606
  16.5 0.0 collective-permute-done.1.refs_2_.refs_5_.refs_3_
  16.5 0.0 collective-permute-done.refs_0_.refs_3_.refs_2_
  16.5 0.2 edges.1
  16.7 3.7 %collective-permute-start.2 = (f32[7,24,128]{2,1,0:T(8,128)S(1)}, f32[7,24,128]{2,1,0:T(8,128)S(1)}, u32[]{:S(2)}, u32[]{:S(2)}) collective-permute-start(f32[7,24,128]{2,1,0:T(8,128)S(1)} %get-tuple-element.8), channel_id=1, source_target_pairs={{0,1},{1,2},{2,3},{3,4},{4,5},{5,6},{6,7},{8,9},{9,10},{10,11},{11... | collective-permute-start | bytes 258056 | tf_op jit(solution)/shard_map/ppermute | solution.py:611
  20.4 1.3 %collective-permute-start.3 = (f32[7,24,128]{2,1,0:T(8,128)S(1)}, f32[7,24,128]{2,1,0:T(8,128)S(1)}, u32[]{:S(2)}, u32[]{:S(2)}) collective-permute-start(f32[7,24,128]{2,1,0:T(8,128)S(1)} %get-tuple-element.9), channel_id=1, source_target_pairs={{1,0},{2,1},{3,2},{4,3},{5,4},{6,5},{7,6},{9,8},{10,9},{11,10},{12... | collective-permute-start | bytes 258056 | tf_op jit(solution)/shard_map/ppermute | solution.py:612
  21.7 0.1 pad_add_fusion.refs_0_
  21.8 8.2 %all-to-all-done.refs_0_ = f32[32,24,128]{2,1,0:T(8,128)S(1)} async-done(((f32[32,24,128]{2,1,0:T(8,128)}), f32[32,24,128]{2,1,0:T(8,128)S(1)}, u32[]{:S(2)}, u32[]{:S(2)}) %all-to-all-start) | async-done | bytes 393248 | tf_op jit(solution)/shard_map/all_to_all | solution.py:606
  30.0 2.4 %add_on_nodes.1 = (f32[5,64,512]{2,1,0:T(8,128)S(1)}, f32[5,64,128]{2,1,0:T(8,128)S(1)}) custom-call(f32[32,24,128]{2,1,0:T(8,128)S(1)} %all-to-all-done.refs_0_), custom_call_target="tpu_custom_call" | custom-call | flops 4000000 | bytes 4000000 | tf_op jit(solution)/shard_map/add_on_nodes/pallas_call | solution.py:183
  32.4 0.0 collective-permute-done.2.refs_4_
  32.4 0.0 collective-permute-done.3.refs_5_
  32.4 0.0 copy-done.2
  32.4 18.7 %solve.1 = (f32[2,32,512]{2,1,0:T(8,128)}, f32[8,128]{1,0:T(8,128)S(1)}) custom-call(s32[2]{0:T(128)S(1)} %pad_add_fusion.refs_0_, f32[7,32,512]{2,1,0:T(8,128)S(1)} %pad_maximum_fusion.refs_1_.refs_4_, f32[7,32,512]{2,1,0:T(8,128)S(1)} %collective-permute-done.refs_0_.refs_3_.refs_2_, f32[7,32,512]{2,1,0:T(8,128)S(1)} %collective-permute-done.1.refs_2_.refs_5_.refs_3_, ...), custom_call_target="tpu_custom_call" | custom-call | flops 80000000 | bytes 4000000 | tf_op jit(solution)/shard_map/solve/pallas_call | solution.py:540
  51.1 1.3 %collective-permute-start.4 = (f32[4,128]{1,0:T(4,128)S(1)}, f32[4,128]{1,0:T(4,128)S(1)}, u32[]{:S(2)}, u32[]{:S(2)}) collective-permute-start(f32[4,128]{1,0:T(4,128)S(1)} %bitcast.20), channel_id=1, source_target_pairs={{0,1},{1,0},{2,3},{3,2},{4,5},{5,4},{6,7},{7,6},{8,9},{9,8},{10,11... | collective-permute-start | bytes 6152 | tf_op jit(solution)/shard_map/ppermute | solution.py:582
  52.4 2.4 %collective-permute-done.4 = f32[4,128]{1,0:T(4,128)S(1)} collective-permute-done((f32[4,128]{1,0:T(4,128)S(1)}, f32[4,128]{1,0:T(4,128)S(1)}, u32[]{:S(2)}, u32[]{:S(2)}) %collective-permute-start.4) | collective-permute-done | bytes 2080 | tf_op jit(solution)/shard_map/ppermute | solution.py:582
  54.8 0.9 %collective-permute-start.5 = (f32[2,128]{1,0:T(2,128)S(1)}, f32[2,128]{1,0:T(2,128)S(1)}, u32[]{:S(2)}, u32[]{:S(2)}) collective-permute-start(f32[2,128]{1,0:T(2,128)S(1)} %bitcast.21), channel_id=1, source_target_pairs={{0,2},{1,3},{2,0},{3,1},{4,6},{5,7},{6,4},{7,5},{8,10},{9,11},{10,... | collective-permute-start | bytes 3080 | tf_op jit(solution)/shard_map/ppermute | solution.py:582
  55.7 2.7 %collective-permute-done.5 = f32[2,128]{1,0:T(2,128)S(1)} collective-permute-done((f32[2,128]{1,0:T(2,128)S(1)}, f32[2,128]{1,0:T(2,128)S(1)}, u32[]{:S(2)}, u32[]{:S(2)}) %collective-permute-start.5) | collective-permute-done | bytes 1056 | tf_op jit(solution)/shard_map/ppermute | solution.py:582
  58.4 0.1 collective-permute-start.6
  58.5 4.4 %collective-permute-done.6 = f32[1,128]{1,0:T(1,128)S(1)} collective-permute-done((f32[1,128]{1,0:T(1,128)S(1)}, f32[1,128]{1,0:T(1,128)S(1)}, u32[]{:S(2)}, u32[]{:S(2)}) %collective-permute-start.6) | collective-permute-done | bytes 544 | tf_op jit(solution)/shard_map/ppermute | solution.py:582
  62.9 0.5 fusion.1
  (6 shorter events, 0.0 us)
Async XLA Ops:
  0.6 5.6 %copy-start.1 = (f32[512,256]{1,0:T(8,128)S(1)}, f32[512,256]{1,0:T(8,128)}, u32[]{:S(2)}) copy-start(f32[512,256]{1,0:T(8,128)} %refs_1_.1) | copy-start | bytes 1572868
  0.6 5.6 %copy-start.4 = (s32[512]{0:T(512)S(1)}, s32[512]{0:T(512)}, u32[]{:S(2)}) copy-start(s32[512]{0:T(512)} %param.17) | copy-start | bytes 6148
  1.8 4.4 %copy-start.3 = (s32[512,1]{0,1:T(1,128)S(1)}, s32[512,1]{0,1:T(1,128)}, u32[]{:S(2)}) copy-start(s32[512,1]{0,1:T(1,128)} %param.16) | copy-start | bytes 6148
  1.8 14.7 %collective-permute-start.1 = (f32[7,32,512]{2,1,0:T(8,128)S(1)}, f32[7,32,512]{2,1,0:T(8,128)S(1)}, u32[]{:S(2)}, u32[]{:S(2)}) collective-permute-start(f32[7,32,512]{2,1,0:T(8,128)S(1)} %pad_maximum_fusion.refs_1_.refs_4_), channel_id=1, source_target_pairs={{8,0},{16,8},{24,16},{9,1},{17,9},{25,17},{10,2},{18,10},{26,18},{... | collective-permute-start | bytes 1376264 | tf_op jit(solution)/shard_map/ppermute | solution.py:27
  3.1 13.4 %collective-permute-start = (f32[7,32,512]{2,1,0:T(8,128)S(1)}, f32[7,32,512]{2,1,0:T(8,128)S(1)}, u32[]{:S(2)}, u32[]{:S(2)}) collective-permute-start(f32[7,32,512]{2,1,0:T(8,128)S(1)} %pad_maximum_fusion.refs_1_.refs_4_), channel_id=1, source_target_pairs={{0,8},{8,16},{16,24},{1,9},{9,17},{17,25},{2,10},{10,18},{18,26},{... | collective-permute-start | bytes 1376264 | tf_op jit(solution)/shard_map/ppermute | solution.py:27
  6.2 1.2 %copy-start = (f32[2,512,256]{2,1,0:T(8,128)S(1)}, f32[2,512,256]{2,1,0:T(8,128)}, u32[]{:S(2)}) copy-start(f32[2,512,256]{2,1,0:T(8,128)} %refs_0_.1) | copy-start | bytes 3145732
  9.2 20.8 %all-to-all-start = ((f32[32,24,128]{2,1,0:T(8,128)}), f32[32,24,128]{2,1,0:T(8,128)S(1)}, u32[]{:S(2)}, u32[]{:S(2)}) async-start(f32[32,24,128]{2,1,0:T(8,128)} %row_sums.1), calls=%async_computation | async-start | bytes 786432 | tf_op jit(solution)/shard_map/all_to_all | solution.py:606
  16.7 15.7 %collective-permute-start.2 = (f32[7,24,128]{2,1,0:T(8,128)S(1)}, f32[7,24,128]{2,1,0:T(8,128)S(1)}, u32[]{:S(2)}, u32[]{:S(2)}) collective-permute-start(f32[7,24,128]{2,1,0:T(8,128)S(1)} %get-tuple-element.8), channel_id=1, source_target_pairs={{0,1},{1,2},{2,3},{3,4},{4,5},{5,6},{6,7},{8,9},{9,10},{10,11},{11... | collective-permute-start | bytes 258056 | tf_op jit(solution)/shard_map/ppermute | solution.py:611
  20.4 12.0 %collective-permute-start.3 = (f32[7,24,128]{2,1,0:T(8,128)S(1)}, f32[7,24,128]{2,1,0:T(8,128)S(1)}, u32[]{:S(2)}, u32[]{:S(2)}) collective-permute-start(f32[7,24,128]{2,1,0:T(8,128)S(1)} %get-tuple-element.9), channel_id=1, source_target_pairs={{1,0},{2,1},{3,2},{4,3},{5,4},{6,5},{7,6},{9,8},{10,9},{11,10},{12... | collective-permute-start | bytes 258056 | tf_op jit(solution)/shard_map/ppermute | solution.py:612
  21.8 10.6 %copy-start.2 = (s32[32,512]{1,0:T(8,128)S(1)}, s32[32,512]{1,0:T(8,128)}, u32[]{:S(2)}) copy-start(s32[32,512]{1,0:T(8,128)} %refs_8_.1) | copy-start | bytes 196612
  51.1 3.7 %collective-permute-start.4 = (f32[4,128]{1,0:T(4,128)S(1)}, f32[4,128]{1,0:T(4,128)S(1)}, u32[]{:S(2)}, u32[]{:S(2)}) collective-permute-start(f32[4,128]{1,0:T(4,128)S(1)} %bitcast.20), channel_id=1, source_target_pairs={{0,1},{1,0},{2,3},{3,2},{4,5},{5,4},{6,7},{7,6},{8,9},{9,8},{10,11... | collective-permute-start | bytes 6152 | tf_op jit(solution)/shard_map/ppermute | solution.py:582
  54.8 3.6 %collective-permute-start.5 = (f32[2,128]{1,0:T(2,128)S(1)}, f32[2,128]{1,0:T(2,128)S(1)}, u32[]{:S(2)}, u32[]{:S(2)}) collective-permute-start(f32[2,128]{1,0:T(2,128)S(1)} %bitcast.21), channel_id=1, source_target_pairs={{0,2},{1,3},{2,0},{3,1},{4,6},{5,7},{6,4},{7,5},{8,10},{9,11},{10,... | collective-permute-start | bytes 3080 | tf_op jit(solution)/shard_map/ppermute | solution.py:582
  58.4 4.5 %collective-permute-start.6 = (f32[1,128]{1,0:T(1,128)S(1)}, f32[1,128]{1,0:T(1,128)S(1)}, u32[]{:S(2)}, u32[]{:S(2)}) collective-permute-start(f32[1,128]{1,0:T(1,128)S(1)} %constant_dynamic-slice_fusion), channel_id=1, source_target_pairs={{0,4},{1,5},{2,6},{3,7},{4,0},{5,1},{6,2},{7,3},{8,12},{9,13},{10,... | collective-permute-start | bytes 1544 | tf_op jit(solution)/shard_map/ppermute | solution.py:582

commit v4 on v3

--- a/solution.py
+++ b/solution.py
@@ -20,11 +20,9 @@
 NT = (((1,), (1,)), ((), ()))
 
 
-def halo_pair(block, axis):
-    count = lax.axis_size(axis)
-    forward = [(i, i + 1) for i in range(count - 1)]
-    backward = [(target, source) for source, target in forward]
-    return lax.ppermute(block, axis, forward), lax.ppermute(block, axis, backward)
+def swap_pairs(block, axis, first):
+    pairs = [(i, i + 1) for i in range(first, lax.axis_size(axis) - 1, 2)]
+    return lax.ppermute(block, axis, pairs + [(b, a) for a, b in pairs])
 
 
 def thirds(values):
@@ -81,6 +79,10 @@
     pad_ref[:, LANES : LANES + devices * cap] = table
     pad_ref[:, LANES + devices * cap :] = edge
     lane8 = lax.broadcasted_iota(jnp.int32, (8, LANES), 1)
+    row8 = lax.broadcasted_iota(jnp.int32, (8, LANES), 0)
+    tail = (lane8 >= 3 * cap) & (lane8 < 4 * cap) & (row8 < 6)
+    packed = tail | (row8 >= 6)
+    pieces = {}
     for g in range(groups):
         for t in range(tiles):
             start = (g * tiles + t - 1) * cap + LANES
@@ -96,13 +98,24 @@
             low = cap if t == 0 else 0
             high = 2 * cap if t == tiles - 1 else 3 * cap
             piece = jnp.where((lane8 >= low) & (lane8 < high), piece, 0.0)
-            for d in range(3):
-                goal = g - (d - 1)
-                if 0 <= goal < groups:
-                    out_ref[goal * tiles + t, d * 8 : d * 8 + 8, :] = piece
-    for t in range(tiles):
-        out_ref[t, 0:8, :] = edge
-        out_ref[(groups - 1) * tiles + t, 16:24, :] = edge
+            turned = jnp.where(row8 < 6, pltpu.roll(piece, 3 * cap, 1), 0.0)
+            shared = jnp.where(row8 < 6, pltpu.roll(piece, 2 * cap, 1), 0.0)
+            for f in range(6):
+                spread = jnp.broadcast_to(piece[f : f + 1], (8, LANES))
+                spread = pltpu.roll(spread, (f % 4 - 2) * cap % LANES, 1) if f % 4 != 2 else spread
+                group = (lane8 >= f % 4 * cap) & (lane8 < f % 4 * cap + cap) & (row8 == 6 + f // 4)
+                turned = jnp.where(group, spread, turned)
+            pieces[g, t] = piece, turned, shared
+    for g in range(groups):
+        for t in range(tiles):
+            top = pieces[g - 1, t][0] if g else edge
+            low = pieces[g, t][0]
+            if g < groups - 1:
+                _, turned, shared = pieces[g + 1, t]
+                top = jnp.where(packed, turned, top)
+                low = jnp.where(tail, shared, low)
+            out_ref[g * tiles + t, 0:8, :] = top
+            out_ref[g * tiles + t, 8:16, :] = low
 
 
 def pack_rows(groups, tiles, look, observed, row_owner, row_cell):
@@ -111,7 +124,7 @@
     cap = max(2, 2 * rows // devices)
     return pl.pallas_call(
         lambda *refs: rows_kernel(groups, tiles, cap, *refs),
-        out_shape=jax.ShapeDtypeStruct((devices, 24, LANES), jnp.float32),
+        out_shape=jax.ShapeDtypeStruct((devices, 16, LANES), jnp.float32),
         scratch_shapes=[pltpu.VMEM((8, devices * cap + 2 * LANES), jnp.float32)],
         compiler_params=pltpu.CompilerParams(vmem_limit_bytes=12 * MIB),
         cost_estimate=pl.CostEstimate(flops=4_000_000, bytes_accessed=80_000_000, transcendentals=0),
@@ -125,6 +138,7 @@
     slots = devices * cap
     shift = rows_y.bit_length() - 1
     lane8 = lax.broadcasted_iota(jnp.int32, (8, LANES), 1)
+    row8 = lax.broadcasted_iota(jnp.int32, (8, LANES), 0)
     for d in range(3):
         wide = rows_x if d == 1 else STRIP
         first_x = {0: rows_x - STRIP, 1: 0, 2: 0}[d]
@@ -135,10 +149,20 @@
             for j in range(devices // per):
                 part = jnp.zeros((8, LANES), jnp.float32)
                 for q in range(per):
-                    source = in_ref[j * per + q, d * 8 : d * 8 + 8, :]
-                    turn = (q - dt) * cap % LANES
+                    here = (lane8 >= q * cap) & (lane8 < q * cap + cap)
+                    if d == 2 and dt == 2:
+                        for f in range(6):
+                            source = in_ref[j * per + q, 6 + f // 4 : 7 + f // 4, :]
+                            moved = jnp.broadcast_to(source, (8, LANES))
+                            turn = (q - f % 4) * cap % LANES
+                            moved = pltpu.roll(moved, turn, 1) if turn else moved
+                            part = jnp.where(here & (row8 == f), moved, part)
+                        continue
+                    at = 8 * dt if d == 2 else 8 * d
+                    source = in_ref[j * per + q, at : at + 8, :]
+                    turn = (q - (3 if d == 2 else dt)) * cap % LANES
                     moved = pltpu.roll(source, turn, 1) if turn else source
-                    part = jnp.where((lane8 >= q * cap) & (lane8 < q * cap + cap), moved, part)
+                    part = jnp.where(here & (row8 < 6), moved, part)
                 parts.append(part)
             lists.append(jnp.concatenate(parts, axis=1))
         for where, out_ref, width in (((1,), mid_ref, rows_y), ((0, 2), side_ref, LANES)):
@@ -196,29 +220,35 @@
     )(arrived)
 
 
-def edges_kernel(*refs):
-    heads, tails, (to_low_ref, to_high_ref) = refs[:3], refs[3:6], refs[6:]
+def edges_kernel(place_ref, *refs):
+    heads, tails, (even_ref, odd_ref) = refs[:3], refs[3:6], refs[6:]
     lane = lax.broadcasted_iota(jnp.int32, (8, LANES), 1)
+    odd_grp = jnp.broadcast_to(place_ref[0] % 2 == 1, lane.shape)
+    odd_tile = jnp.broadcast_to(place_ref[1] % 2 == 1, lane.shape)
+
+    def pick(parts, block, f):
+        own, even, odd = [part[f, block % 4 * 8 : block % 4 * 8 + 8, :] for part in parts]
+        return (jnp.where(odd_grp, even, odd), own, jnp.where(odd_grp, odd, even))[block // 4]
+
     for f in range(FIELDS):
         for b in range(3):
             begin = jnp.zeros((8, LANES), jnp.float32)
             end = jnp.zeros((8, LANES), jnp.float32)
             for k in range(4):
                 block = 3 * k + b
-                at = block % 4 * 8
                 mine = (lane >= 32 * k) & (lane < 32 * k + 32)
-                head, tail = heads[block // 4][f, at : at + 8, :], tails[block // 4][f, at : at + 8, :]
+                head, tail = pick(heads, block, f), pick(tails, block, f)
                 if k:
                     head = pltpu.roll(head, 32 * k, 1)
                 if k != 3:
                     tail = pltpu.roll(tail, 32 * k + 32, 1)
                 begin = jnp.where(mine, head, begin)
                 end = jnp.where(mine, tail, end)
-            to_low_ref[f, b * 8 : b * 8 + 8, :] = begin
-            to_high_ref[f, b * 8 : b * 8 + 8, :] = end
-
-
-def edges(low, own, high):
+            even_ref[f, b * 8 : b * 8 + 8, :] = jnp.where(odd_tile, begin, end)
+            odd_ref[f, b * 8 : b * 8 + 8, :] = jnp.where(odd_tile, end, begin)
+
+
+def edges(place, own, even, odd):
     shape = jax.ShapeDtypeStruct((FIELDS, 24, LANES), jnp.float32)
     part = (FIELDS, own.shape[1], LANES)
     last = own.shape[2] // LANES - 1
@@ -228,13 +258,13 @@
     return pl.pallas_call(
         edges_kernel,
         grid=(1,),
-        in_specs=[head] * 3 + [tail] * 3,
+        in_specs=[pl.BlockSpec(memory_space=pltpu.SMEM)] + [head] * 3 + [tail] * 3,
         out_specs=(whole, whole),
         out_shape=(shape, shape),
         compiler_params=pltpu.CompilerParams(vmem_limit_bytes=4 * MIB),
         cost_estimate=pl.CostEstimate(flops=100_000_000_000, bytes_accessed=500_000, transcendentals=0),
         name="edges",
-    )(low, own, high, low, own, high)
+    )(place, own, even, odd, own, even, odd)
 
 
 def tile_rows(row, count=1):
@@ -310,10 +340,10 @@
     tile_count,
     place_ref,
     own_ref,
-    low_ref,
-    high_ref,
-    left_ref,
-    right_ref,
+    grp_even_ref,
+    grp_odd_ref,
+    tile_even_ref,
+    tile_odd_ref,
     mid_ref,
     side_ref,
     ids_ref,
@@ -338,13 +368,23 @@
     height = rows_x + 2 * REACH
     grp, tile = place_ref[0], place_ref[1]
 
-    sources = (low_ref, own_ref, high_ref)
+    odd_grp = jnp.broadcast_to(grp % 2 == 1, (8, LANES))
+    odd_tile = jnp.broadcast_to(tile % 2 == 1, (8, LANES))
+
+    def pick(f, block, j):
+        at = (f, slice(block % 4 * 8, block % 4 * 8 + 8), slice(LANES * j, LANES * j + LANES))
+        if block // 4 == 1:
+            return own_ref[at]
+        even, odd = grp_even_ref[at], grp_odd_ref[at]
+        return jnp.where(odd_grp, even, odd) if block < 4 else jnp.where(odd_grp, odd, even)
+
     for f in range(FIELDS):
         for block in range(height // 8):
-            ref, at = sources[block // 4], block % 4 * 8
             k, b = block // 3, block % 3
-            left = left_ref[f, b * 8 : b * 8 + 8, :]
-            right = right_ref[f, b * 8 : b * 8 + 8, :]
+            even = tile_even_ref[f, b * 8 : b * 8 + 8, :]
+            odd = tile_odd_ref[f, b * 8 : b * 8 + 8, :]
+            left = jnp.where(odd_tile, even, odd)
+            right = jnp.where(odd_tile, odd, even)
             if k:
                 left = pltpu.roll(left, LANES - 32 * k, 1)
             if k != 3:
@@ -353,7 +393,7 @@
             def store(s, value, f=f, block=block):
                 field[f, pl.ds(64 * block + s, 8, stride=8), :] = value
 
-            to_rows([ref[f, at : at + 8, LANES * j : LANES * j + LANES] for j in range(4)], left, right, store)
+            to_rows([pick(f, block, j) for j in range(4)], left, right, store)
     for f in range(5):
         for block in range((rows_x + 2 * STRIP) // 8):
             at = block * 8
@@ -530,7 +570,7 @@
     elem_ref[...] = sums[:owners] + sums[owners : 2 * owners] + sums[2 * owners :]
 
 
-def solve(place, own, low, high, left, right, mid, side, ids, epochs, grp_count, tile_count):
+def solve(place, own, grp_halos, tile_halos, mid, side, ids, epochs, grp_count, tile_count):
     rows_x, rows_y = ids.shape
     height = rows_x + 2 * REACH
     elems = LANES
@@ -566,7 +606,7 @@
             flops=80_000_000, bytes_accessed=4_000_000, transcendentals=0
         ),
         name="solve",
-    )(place, own, low, high, left, right, mid, side, ids)
+    )(place, own, *grp_halos, *tile_halos, mid, side, ids)
 
 
 def sum_onto_owner(terms, axis):
@@ -601,19 +641,15 @@
     devices = groups * tiles
     cap = max(2, 2 * row_dev // devices)
     own = jnp.concatenate([start_velocity, driving_stress, viscosity, friction[None]], axis=0)
-    low, high = halo_pair(own, "grp")
+    place = jnp.stack([lax.axis_index("grp"), lax.axis_index("tile")]).astype(jnp.int32)
+    grp_halos = [swap_pairs(own, "grp", first) for first in (0, 1)]
     outgoing = pack_rows(groups, tiles, look, observed, row_owner, row_cell)
     arrived = lax.all_to_all(outgoing, ("grp", "tile"), split_axis=0, concat_axis=0, tiled=True)
-    to_low, to_high = edges(low, own, high)
-    count = tiles
-    forward = [(i, i + 1) for i in range(count - 1)]
-    backward = [(target, source) for source, target in forward]
-    left = lax.ppermute(to_high, "tile", forward)
-    right = lax.ppermute(to_low, "tile", backward)
+    sent = edges(place, own, *grp_halos)
+    tile_halos = [swap_pairs(block, "tile", first) for first, block in enumerate(sent)]
     mid, side = add_on_nodes(arrived, cap, rows_x, rows_y)
-    place = jnp.stack([lax.axis_index("grp"), lax.axis_index("tile")]).astype(jnp.int32)
     stress_adjoint, terms = solve(
-        place, own, low, high, left, right, mid, side, cell_element, epochs, groups, tiles
+        place, own, grp_halos, tile_halos, mid, side, cell_element, epochs, groups, tiles
     )
     return stress_adjoint, sum_onto_owner(terms, "tile")
 

time: 63.8 us -> 59.3 us (0.929)
  starting transfers between devices: 18.9 us -> 15.7 us
  waiting for transfers between devices: 17.7 us -> 15.8 us
  Pallas kernels: 23 us -> 23.7 us
    ppermute x4, starting transfers between devices: 9.32 us -> 3.68 us  [swap_pairs(): return lax.ppermute(block, axis, pairs + [(b, a) for a, b in pairs])]
    all_to_all x1, starting transfers between devices: 7.3 us -> 8.71 us  [shards(): lax.all_to_all(outgoing, ('grp', 'tile'), split_axis=0, concat_axis=0, ti...]
    ppermute x3, starting transfers between devices: 2.26 us -> 3.26 us  [sum_onto_owner(): lax.ppermute(other, axis, [(i, i ^ span) for i in range(count)])]
    ppermute x3, waiting for transfers between devices: 9.51 us -> 8.52 us  [sum_onto_owner(): lax.ppermute(other, axis, [(i, i ^ span) for i in range(count)])]
    all_to_all x1, waiting for transfers between devices: 8.23 us -> 7.28 us  [shards(): lax.all_to_all(outgoing, ('grp', 'tile'), split_axis=0, concat_axis=0, ti...]
  transfers between devices with their start and end apart: 8 -> 8, of which waited for: 4 -> 4; matrix products, arithmetic and copies ran while one was open for 0% -> 0% of each run, Pallas kernels for 7% -> 8%
where the time goes in v4:
time: 59.3 us; the launch traced here: 59 us
  Pallas kernels  23.7 us (40%)
  waiting for transfers between devices  15.8 us (27%)
  starting transfers between devices  15.7 us (26%)
  other arithmetic  1.75 us (3%)
  local copies, waits for them, and re-layouts  1.27 us (2%)
  between operations  0.8 us (1%)
    pallas_call x1, Pallas kernels, solve(): pl.pallas_call(lambda *refs: solve_kernel(epochs, grp_count, tile_count,...  18.7 us
    all_to_all x1, starting transfers between devices, shards(): lax.all_to_all(outgoing, ('grp', 'tile'), split_axis=0, concat_axis=0, ti...  8.71 us
    ppermute x3, waiting for transfers between devices, sum_onto_owner(): lax.ppermute(other, axis, [(i, i ^ span) for i in range(count)])  8.52 us
    all_to_all x1, waiting for transfers between devices, shards(): lax.all_to_all(outgoing, ('grp', 'tile'), split_axis=0, concat_axis=0, ti...  7.28 us
    ppermute x4, starting transfers between devices, swap_pairs(): return lax.ppermute(block, axis, pairs + [(b, a) for a, b in pairs])  3.68 us
    ppermute x3, starting transfers between devices, sum_onto_owner(): lax.ppermute(other, axis, [(i, i ^ span) for i in range(count)])  3.26 us
    pallas_call x1, Pallas kernels, add_on_nodes(): pl.pallas_call(lambda *refs: nodes_kernel(cap, rows_x, rows_y, *refs), ou...  2.37 us
    pallas_call x1, Pallas kernels, pack_rows(): pl.pallas_call(lambda *refs: rows_kernel(groups, tiles, cap, *refs), out_...  1.9 us
  transfers between devices with their start and end apart: 8, of which 4 were waited for; matrix products, arithmetic and copies ran while one was open for 0% of the time, Pallas kernels for 8%

profile of v4, /device:TPU:0, one launch (start us, length us, event | category | flops | bytes accessed | tf_op | source)
XLA Modules:
  0.0 59.0 jit_solution(3050243011580403260)
XLA Ops:
  0.6 0.0 copy-start.1
  0.6 0.0 copy-start.4
  0.7 1.1 %pad_maximum_fusion.refs_0_.refs_3_.refs_1_ = f32[7,32,512]{2,1,0:T(8,128)S(1)} fusion(f32[1,32,512]{2,1,0:T(8,128)} %bitcast.16, f32[2,32,512]{2,1,0:T(8,128)} %param.11, f32[2,32,512]{2,1,0:T(8,128)} %param.10, f32[2,32,512]{2,1,0:T(8,128)} %param.9), kind=kLoop, calls=%fused_computation | loop fusion | flops 344064 | bytes 917504 | tf_op jit(solution)/shard_map/concatenate | solution.py:643
  1.8 0.0 copy-start.3
  1.8 0.5 collective-permute-start
  2.3 0.7 %collective-permute-start.1 = (f32[7,32,512]{2,1,0:T(8,128)S(1)}, f32[7,32,512]{2,1,0:T(8,128)S(1)}, u32[]{:S(2)}, u32[]{:S(2)}) collective-permute-start(f32[7,32,512]{2,1,0:T(8,128)S(1)} %pad_maximum_fusion.refs_0_.refs_3_.refs_1_), channel_id=1, source_target_pairs={{8,16},{16,8},{9,17},{17,9},{10,18},{18,10},{11,19},{19,11},{12,20... | collective-permute-start | bytes 1376264 | tf_op jit(solution)/shard_map/ppermute | solution.py:25
  3.0 0.0 copy-done.1
  3.0 0.0 copy-done.4
  3.1 0.0 copy-start
  3.1 1.2 %copy-done = f32[2,512,256]{2,1,0:T(8,128)S(1)} copy-done((f32[2,512,256]{2,1,0:T(8,128)S(1)}, f32[2,512,256]{2,1,0:T(8,128)}, u32[]{:S(2)}) %copy-start) | copy-done | bytes 1048600
  4.3 1.9 %row_sums.1 = f32[32,16,128]{2,1,0:T(8,128)} custom-call(f32[2,512,256]{2,1,0:T(8,128)S(1)} %copy-done, f32[512,256]{1,0:T(8,128)S(1)} %copy-done.1, s32[1,512]{1,0:T(1,128)S(1)} %bitcast.14, s32[1,512]{1,0:T(1,128)S(1)} %bitcast.15), custom_call_target="tpu_custom_call" | custom-call | flops 4000000 | bytes 80000000 | tf_op jit(solution)/shard_map/row_sums/pallas_call | solution.py:125
  6.2 8.7 %all-to-all-start = ((f32[32,16,128]{2,1,0:T(8,128)}), f32[32,16,128]{2,1,0:T(8,128)S(1)}, u32[]{:S(2)}, u32[]{:S(2)}) async-start(f32[32,16,128]{2,1,0:T(8,128)} %row_sums.1), calls=%async_computation | async-start | bytes 524288 | tf_op jit(solution)/shard_map/all_to_all | solution.py:647
  14.9 0.1 pad_add_fusion.place_ref.refs_0_
  15.0 0.0 collective-permute-done.refs_1_.refs_4_.refs_2_
  15.0 0.0 collective-permute-done.1.refs_2_.refs_5_.refs_3_
  15.0 0.7 %edges.1 = (f32[7,24,128]{2,1,0:T(8,128)S(1)}, f32[7,24,128]{2,1,0:T(8,128)S(1)}) custom-call(s32[2]{0:T(128)S(1)} %pad_add_fusion.place_ref.refs_0_, f32[7,32,512]{2,1,0:T(8,128)S(1)} %pad_maximum_fusion.refs_0_.refs_3_.refs_1_, f32[7,32,512]{2,1,0:T(8,128)S(1)} %collective-permute-done.refs_1_.refs_4_.refs_2_, ...), custom_call_target="tpu_custom_call" | custom-call | flops 99999997952 | bytes 500000 | tf_op jit(solution)/shard_map/edges/pallas_call | solution.py:258
  15.7 1.8 %collective-permute-start.2 = (f32[7,24,128]{2,1,0:T(8,128)S(1)}, f32[7,24,128]{2,1,0:T(8,128)S(1)}, u32[]{:S(2)}, u32[]{:S(2)}) collective-permute-start(f32[7,24,128]{2,1,0:T(8,128)S(1)} %get-tuple-element.8), channel_id=1, source_target_pairs={{0,1},{2,3},{4,5},{6,7},{1,0},{3,2},{5,4},{7,6},{8,9},{10,11},{12,... | collective-permute-start | bytes 258056 | tf_op jit(solution)/shard_map/ppermute | solution.py:25
  17.6 0.7 %collective-permute-start.3 = (f32[7,24,128]{2,1,0:T(8,128)S(1)}, f32[7,24,128]{2,1,0:T(8,128)S(1)}, u32[]{:S(2)}, u32[]{:S(2)}) collective-permute-start(f32[7,24,128]{2,1,0:T(8,128)S(1)} %get-tuple-element.9), channel_id=1, source_target_pairs={{1,2},{3,4},{5,6},{2,1},{4,3},{6,5},{9,10},{11,12},{13,14},{10,9},... | collective-permute-start | bytes 258056 | tf_op jit(solution)/shard_map/ppermute | solution.py:25
  18.3 0.0 copy-start.2
  18.3 7.3 %all-to-all-done.refs_0_ = f32[32,16,128]{2,1,0:T(8,128)S(1)} async-done(((f32[32,16,128]{2,1,0:T(8,128)}), f32[32,16,128]{2,1,0:T(8,128)S(1)}, u32[]{:S(2)}, u32[]{:S(2)}) %all-to-all-start) | async-done | bytes 262176 | tf_op jit(solution)/shard_map/all_to_all | solution.py:647
  25.5 2.4 %add_on_nodes.1 = (f32[5,64,512]{2,1,0:T(8,128)S(1)}, f32[5,64,128]{2,1,0:T(8,128)S(1)}) custom-call(f32[32,16,128]{2,1,0:T(8,128)S(1)} %all-to-all-done.refs_0_), custom_call_target="tpu_custom_call" | custom-call | flops 4000000 | bytes 4000000 | tf_op jit(solution)/shard_map/add_on_nodes/pallas_call | solution.py:207
  27.9 0.0 collective-permute-done.2.refs_4_
  27.9 0.0 collective-permute-done.3.refs_5_
  27.9 0.0 copy-done.2
  28.0 18.7 %solve.1 = (f32[2,32,512]{2,1,0:T(8,128)}, f32[8,128]{1,0:T(8,128)S(1)}) custom-call(s32[2]{0:T(128)S(1)} %pad_add_fusion.place_ref.refs_0_, f32[7,32,512]{2,1,0:T(8,128)S(1)} %pad_maximum_fusion.refs_0_.refs_3_.refs_1_, f32[7,32,512]{2,1,0:T(8,128)S(1)} %collective-permute-done.refs_1_.refs_4_.refs_2_, ...), custom_call_target="tpu_custom_call" | custom-call | flops 80000000 | bytes 4000000 | tf_op jit(solution)/shard_map/solve/pallas_call | solution.py:580
  46.7 1.5 %collective-permute-start.4 = (f32[4,128]{1,0:T(4,128)S(1)}, f32[4,128]{1,0:T(4,128)S(1)}, u32[]{:S(2)}, u32[]{:S(2)}) collective-permute-start(f32[4,128]{1,0:T(4,128)S(1)} %bitcast.20), channel_id=1, source_target_pairs={{0,1},{1,0},{2,3},{3,2},{4,5},{5,4},{6,7},{7,6},{8,9},{9,8},{10,11... | collective-permute-start | bytes 6152 | tf_op jit(solution)/shard_map/ppermute | solution.py:622
  48.2 2.2 %collective-permute-done.4 = f32[4,128]{1,0:T(4,128)S(1)} collective-permute-done((f32[4,128]{1,0:T(4,128)S(1)}, f32[4,128]{1,0:T(4,128)S(1)}, u32[]{:S(2)}, u32[]{:S(2)}) %collective-permute-start.4) | collective-permute-done | bytes 2080 | tf_op jit(solution)/shard_map/ppermute | solution.py:622
  50.4 1.2 %collective-permute-start.5 = (f32[2,128]{1,0:T(2,128)S(1)}, f32[2,128]{1,0:T(2,128)S(1)}, u32[]{:S(2)}, u32[]{:S(2)}) collective-permute-start(f32[2,128]{1,0:T(2,128)S(1)} %bitcast.21), channel_id=1, source_target_pairs={{0,2},{1,3},{2,0},{3,1},{4,6},{5,7},{6,4},{7,5},{8,10},{9,11},{10,... | collective-permute-start | bytes 3080 | tf_op jit(solution)/shard_map/ppermute | solution.py:622
  51.5 2.4 %collective-permute-done.5 = f32[2,128]{1,0:T(2,128)S(1)} collective-permute-done((f32[2,128]{1,0:T(2,128)S(1)}, f32[2,128]{1,0:T(2,128)S(1)}, u32[]{:S(2)}, u32[]{:S(2)}) %collective-permute-start.5) | collective-permute-done | bytes 1056 | tf_op jit(solution)/shard_map/ppermute | solution.py:622
  54.0 0.6 %collective-permute-start.6 = (f32[1,128]{1,0:T(1,128)S(1)}, f32[1,128]{1,0:T(1,128)S(1)}, u32[]{:S(2)}, u32[]{:S(2)}) collective-permute-start(f32[1,128]{1,0:T(1,128)S(1)} %constant_dynamic-slice_fusion), channel_id=1, source_target_pairs={{0,4},{1,5},{2,6},{3,7},{4,0},{5,1},{6,2},{7,3},{8,12},{9,13},{10,... | collective-permute-start | bytes 1544 | tf_op jit(solution)/shard_map/ppermute | solution.py:622
  54.6 3.9 %collective-permute-done.6 = f32[1,128]{1,0:T(1,128)S(1)} collective-permute-done((f32[1,128]{1,0:T(1,128)S(1)}, f32[1,128]{1,0:T(1,128)S(1)}, u32[]{:S(2)}, u32[]{:S(2)}) %collective-permute-start.6) | collective-permute-done | bytes 544 | tf_op jit(solution)/shard_map/ppermute | solution.py:622
  58.5 0.5 fusion.1
  (6 shorter events, 0.0 us)
Async XLA Ops:
  0.6 2.4 %copy-start.1 = (f32[512,256]{1,0:T(8,128)S(1)}, f32[512,256]{1,0:T(8,128)}, u32[]{:S(2)}) copy-start(f32[512,256]{1,0:T(8,128)} %refs_1_.1) | copy-start | bytes 1572868
  0.6 2.4 %copy-start.4 = (s32[512]{0:T(512)S(1)}, s32[512]{0:T(512)}, u32[]{:S(2)}) copy-start(s32[512]{0:T(512)} %param.17) | copy-start | bytes 6148
  1.8 1.2 %copy-start.3 = (s32[512,1]{0,1:T(1,128)S(1)}, s32[512,1]{0,1:T(1,128)}, u32[]{:S(2)}) copy-start(s32[512,1]{0,1:T(1,128)} %param.16) | copy-start | bytes 6148
  1.8 13.2 %collective-permute-start = (f32[7,32,512]{2,1,0:T(8,128)S(1)}, f32[7,32,512]{2,1,0:T(8,128)S(1)}, u32[]{:S(2)}, u32[]{:S(2)}) collective-permute-start(f32[7,32,512]{2,1,0:T(8,128)S(1)} %pad_maximum_fusion.refs_0_.refs_3_.refs_1_), channel_id=1, source_target_pairs={{0,8},{16,24},{8,0},{24,16},{1,9},{17,25},{9,1},{25,17},{2,10},{18... | collective-permute-start | bytes 1376264 | tf_op jit(solution)/shard_map/ppermute | solution.py:25
  2.3 12.7 %collective-permute-start.1 = (f32[7,32,512]{2,1,0:T(8,128)S(1)}, f32[7,32,512]{2,1,0:T(8,128)S(1)}, u32[]{:S(2)}, u32[]{:S(2)}) collective-permute-start(f32[7,32,512]{2,1,0:T(8,128)S(1)} %pad_maximum_fusion.refs_0_.refs_3_.refs_1_), channel_id=1, source_target_pairs={{8,16},{16,8},{9,17},{17,9},{10,18},{18,10},{11,19},{19,11},{12,20... | collective-permute-start | bytes 1376264 | tf_op jit(solution)/shard_map/ppermute | solution.py:25
  3.1 1.2 %copy-start = (f32[2,512,256]{2,1,0:T(8,128)S(1)}, f32[2,512,256]{2,1,0:T(8,128)}, u32[]{:S(2)}) copy-start(f32[2,512,256]{2,1,0:T(8,128)} %refs_0_.1) | copy-start | bytes 3145732
  6.2 19.4 %all-to-all-start = ((f32[32,16,128]{2,1,0:T(8,128)}), f32[32,16,128]{2,1,0:T(8,128)S(1)}, u32[]{:S(2)}, u32[]{:S(2)}) async-start(f32[32,16,128]{2,1,0:T(8,128)} %row_sums.1), calls=%async_computation | async-start | bytes 524288 | tf_op jit(solution)/shard_map/all_to_all | solution.py:647
  15.7 12.2 %collective-permute-start.2 = (f32[7,24,128]{2,1,0:T(8,128)S(1)}, f32[7,24,128]{2,1,0:T(8,128)S(1)}, u32[]{:S(2)}, u32[]{:S(2)}) collective-permute-start(f32[7,24,128]{2,1,0:T(8,128)S(1)} %get-tuple-element.8), channel_id=1, source_target_pairs={{0,1},{2,3},{4,5},{6,7},{1,0},{3,2},{5,4},{7,6},{8,9},{10,11},{12,... | collective-permute-start | bytes 258056 | tf_op jit(solution)/shard_map/ppermute | solution.py:25
  17.6 10.4 %collective-permute-start.3 = (f32[7,24,128]{2,1,0:T(8,128)S(1)}, f32[7,24,128]{2,1,0:T(8,128)S(1)}, u32[]{:S(2)}, u32[]{:S(2)}) collective-permute-start(f32[7,24,128]{2,1,0:T(8,128)S(1)} %get-tuple-element.9), channel_id=1, source_target_pairs={{1,2},{3,4},{5,6},{2,1},{4,3},{6,5},{9,10},{11,12},{13,14},{10,9},... | collective-permute-start | bytes 258056 | tf_op jit(solution)/shard_map/ppermute | solution.py:25
  18.3 9.7 %copy-start.2 = (s32[32,512]{1,0:T(8,128)S(1)}, s32[32,512]{1,0:T(8,128)}, u32[]{:S(2)}) copy-start(s32[32,512]{1,0:T(8,128)} %refs_8_.1) | copy-start | bytes 196612
  46.7 3.7 %collective-permute-start.4 = (f32[4,128]{1,0:T(4,128)S(1)}, f32[4,128]{1,0:T(4,128)S(1)}, u32[]{:S(2)}, u32[]{:S(2)}) collective-permute-start(f32[4,128]{1,0:T(4,128)S(1)} %bitcast.20), channel_id=1, source_target_pairs={{0,1},{1,0},{2,3},{3,2},{4,5},{5,4},{6,7},{7,6},{8,9},{9,8},{10,11... | collective-permute-start | bytes 6152 | tf_op jit(solution)/shard_map/ppermute | solution.py:622
  50.4 3.6 %collective-permute-start.5 = (f32[2,128]{1,0:T(2,128)S(1)}, f32[2,128]{1,0:T(2,128)S(1)}, u32[]{:S(2)}, u32[]{:S(2)}) collective-permute-start(f32[2,128]{1,0:T(2,128)S(1)} %bitcast.21), channel_id=1, source_target_pairs={{0,2},{1,3},{2,0},{3,1},{4,6},{5,7},{6,4},{7,5},{8,10},{9,11},{10,... | collective-permute-start | bytes 3080 | tf_op jit(solution)/shard_map/ppermute | solution.py:622
  54.0 4.5 %collective-permute-start.6 = (f32[1,128]{1,0:T(1,128)S(1)}, f32[1,128]{1,0:T(1,128)S(1)}, u32[]{:S(2)}, u32[]{:S(2)}) collective-permute-start(f32[1,128]{1,0:T(1,128)S(1)} %constant_dynamic-slice_fusion), channel_id=1, source_target_pairs={{0,4},{1,5},{2,6},{3,7},{4,0},{5,1},{6,2},{7,3},{8,12},{9,13},{10,... | collective-permute-start | bytes 1544 | tf_op jit(solution)/shard_map/ppermute | solution.py:622

commit v5 on v4

--- a/solution.py
+++ b/solution.py
@@ -14,7 +14,7 @@
 REACH = 32
 CHUNK = 64
 CHUNKS = 8
-DELAY = 14
+DELAY = 30
 STRIP = 16
 MIB = 1024 * 1024
 NT = (((1,), (1,)), ((), ()))
@@ -220,11 +220,11 @@
     )(arrived)
 
 
-def edges_kernel(place_ref, *refs):
+def edges_kernel(*refs):
     heads, tails, (even_ref, odd_ref) = refs[:3], refs[3:6], refs[6:]
     lane = lax.broadcasted_iota(jnp.int32, (8, LANES), 1)
-    odd_grp = jnp.broadcast_to(place_ref[0] % 2 == 1, lane.shape)
-    odd_tile = jnp.broadcast_to(place_ref[1] % 2 == 1, lane.shape)
+    odd_grp = jnp.broadcast_to(lax.axis_index("grp") % 2 == 1, lane.shape)
+    odd_tile = jnp.broadcast_to(lax.axis_index("tile") % 2 == 1, lane.shape)
 
     def pick(parts, block, f):
         own, even, odd = [part[f, block % 4 * 8 : block % 4 * 8 + 8, :] for part in parts]
@@ -248,7 +248,7 @@
             odd_ref[f, b * 8 : b * 8 + 8, :] = jnp.where(odd_tile, end, begin)
 
 
-def edges(place, own, even, odd):
+def edges(own, even, odd):
     shape = jax.ShapeDtypeStruct((FIELDS, 24, LANES), jnp.float32)
     part = (FIELDS, own.shape[1], LANES)
     last = own.shape[2] // LANES - 1
@@ -258,13 +258,13 @@
     return pl.pallas_call(
         edges_kernel,
         grid=(1,),
-        in_specs=[pl.BlockSpec(memory_space=pltpu.SMEM)] + [head] * 3 + [tail] * 3,
+        in_specs=[head] * 3 + [tail] * 3,
         out_specs=(whole, whole),
         out_shape=(shape, shape),
         compiler_params=pltpu.CompilerParams(vmem_limit_bytes=4 * MIB),
         cost_estimate=pl.CostEstimate(flops=100_000_000_000, bytes_accessed=500_000, transcendentals=0),
         name="edges",
-    )(place, own, even, odd, own, even, odd)
+    )(own, even, odd, own, even, odd)
 
 
 def tile_rows(row, count=1):
@@ -338,7 +338,6 @@
     epochs,
     grp_count,
     tile_count,
-    place_ref,
     own_ref,
     grp_even_ref,
     grp_odd_ref,
@@ -366,7 +365,7 @@
 ):
     rows_x = own_ref.shape[1]
     height = rows_x + 2 * REACH
-    grp, tile = place_ref[0], place_ref[1]
+    grp, tile = lax.axis_index("grp"), lax.axis_index("tile")
 
     odd_grp = jnp.broadcast_to(grp % 2 == 1, (8, LANES))
     odd_tile = jnp.broadcast_to(tile % 2 == 1, (8, LANES))
@@ -460,8 +459,8 @@
             target(1, row, new_v)
             if REACH <= row < REACH + rows_x:
                 here = pl.ds(8 * (row - REACH), 8)
-                seen[step, 0, here, :] = u + (new_u - u) * (1.0 / 0.45)
-                seen[step, 1, here, :] = v + (new_v - v) * (1.0 / 0.45)
+                seen[step, 0, here, :] = new_u - 0.55 * u
+                seen[step, 1, here, :] = new_v - 0.55 * v
 
         stencil_rows(lambda r: source(0, r), lambda r: source(1, r), visc(p), first_row, last_row, finish)
 
@@ -548,7 +547,7 @@
         tiles = from_rows(lambda s: fric[pl.ds(64 * block + s, 8, stride=8), :])
         for k in range(4):
             terms[at, LANES * k : LANES * k + LANES] = (
-                tiles[k] * own_ref[6, at, LANES * k : LANES * k + LANES]
+                tiles[k] * (own_ref[6, at, LANES * k : LANES * k + LANES] * (1.0 / 0.45))
             )
 
     owners, elems = elem_ref.shape
@@ -570,7 +569,7 @@
     elem_ref[...] = sums[:owners] + sums[owners : 2 * owners] + sums[2 * owners :]
 
 
-def solve(place, own, grp_halos, tile_halos, mid, side, ids, epochs, grp_count, tile_count):
+def solve(own, grp_halos, tile_halos, mid, side, ids, epochs, grp_count, tile_count):
     rows_x, rows_y = ids.shape
     height = rows_x + 2 * REACH
     elems = LANES
@@ -579,7 +578,7 @@
     f32 = jnp.float32
     return pl.pallas_call(
         lambda *refs: solve_kernel(epochs, grp_count, tile_count, *refs),
-        in_specs=[pl.BlockSpec(memory_space=pltpu.SMEM)] + [spec] * 8,
+        in_specs=[spec] * 8,
         out_specs=(spec, spec),
         out_shape=(
             jax.ShapeDtypeStruct((2, rows_x, rows_y), f32),
@@ -606,7 +605,7 @@
             flops=80_000_000, bytes_accessed=4_000_000, transcendentals=0
         ),
         name="solve",
-    )(place, own, *grp_halos, *tile_halos, mid, side, ids)
+    )(own, *grp_halos, *tile_halos, mid, side, ids)
 
 
 def sum_onto_owner(terms, axis):
@@ -641,15 +640,14 @@
     devices = groups * tiles
     cap = max(2, 2 * row_dev // devices)
     own = jnp.concatenate([start_velocity, driving_stress, viscosity, friction[None]], axis=0)
-    place = jnp.stack([lax.axis_index("grp"), lax.axis_index("tile")]).astype(jnp.int32)
     grp_halos = [swap_pairs(own, "grp", first) for first in (0, 1)]
     outgoing = pack_rows(groups, tiles, look, observed, row_owner, row_cell)
     arrived = lax.all_to_all(outgoing, ("grp", "tile"), split_axis=0, concat_axis=0, tiled=True)
-    sent = edges(place, own, *grp_halos)
+    sent = edges(own, *grp_halos)
     tile_halos = [swap_pairs(block, "tile", first) for first, block in enumerate(sent)]
     mid, side = add_on_nodes(arrived, cap, rows_x, rows_y)
     stress_adjoint, terms = solve(
-        place, own, grp_halos, tile_halos, mid, side, cell_element, epochs, groups, tiles
+        own, grp_halos, tile_halos, mid, side, cell_element, epochs, groups, tiles
     )
     return stress_adjoint, sum_onto_owner(terms, "tile")
 

time: 59.3 us -> 56.8 us (0.958)
  Pallas kernels: 23.7 us -> 20.8 us
  waiting for transfers between devices: 15.8 us -> 16.6 us
    pallas_call x1, Pallas kernels: 18.7 us -> 16.3 us  [solve(): pl.pallas_call(lambda *refs: solve_kernel(epochs, grp_count, tile_count,...]
    all_to_all x1, waiting for transfers between devices: 7.28 us -> 7.88 us  [shards(): lax.all_to_all(outgoing, ('grp', 'tile'), split_axis=0, concat_axis=0, ti...]
where the time goes in v5:
time: 56.8 us; the launch traced here: 56.6 us
  Pallas kernels  20.8 us (37%)
  waiting for transfers between devices  16.6 us (29%)
  starting transfers between devices  15.5 us (27%)
  other arithmetic  1.67 us (3%)
  local copies, waits for them, and re-layouts  1.27 us (2%)
  between operations  0.81 us (1%)
    pallas_call x1, Pallas kernels, solve(): pl.pallas_call(lambda *refs: solve_kernel(epochs, grp_count, tile_count,...  16.3 us
    all_to_all x1, starting transfers between devices, shards(): lax.all_to_all(outgoing, ('grp', 'tile'), split_axis=0, concat_axis=0, ti...  8.71 us
    ppermute x3, waiting for transfers between devices, sum_onto_owner(): lax.ppermute(other, axis, [(i, i ^ span) for i in range(count)])  8.69 us
    all_to_all x1, waiting for transfers between devices, shards(): lax.all_to_all(outgoing, ('grp', 'tile'), split_axis=0, concat_axis=0, ti...  7.88 us
    ppermute x4, starting transfers between devices, swap_pairs(): return lax.ppermute(block, axis, pairs + [(b, a) for a, b in pairs])  3.68 us
    ppermute x3, starting transfers between devices, sum_onto_owner(): lax.ppermute(other, axis, [(i, i ^ span) for i in range(count)])  3.1 us
    pallas_call x1, Pallas kernels, add_on_nodes(): pl.pallas_call(lambda *refs: nodes_kernel(cap, rows_x, rows_y, *refs), ou...  2.37 us
    pallas_call x1, Pallas kernels, pack_rows(): pl.pallas_call(lambda *refs: rows_kernel(groups, tiles, cap, *refs), out_...  1.9 us
  transfers between devices with their start and end apart: 8, of which 4 were waited for; matrix products, arithmetic and copies ran while one was open for 0% of the time, Pallas kernels for 8%

profile of v5, /device:TPU:0, one launch (start us, length us, event | category | flops | bytes accessed | tf_op | source)
XLA Modules:
  0.0 56.6 jit_solution(5332314777254354677)
XLA Ops:
  0.6 0.0 copy-start.1
  0.6 0.0 copy-start.4
  0.7 1.1 %pad_maximum_fusion.refs_0_.refs_3_ = f32[7,32,512]{2,1,0:T(8,128)S(1)} fusion(f32[1,32,512]{2,1,0:T(8,128)} %bitcast.14, f32[2,32,512]{2,1,0:T(8,128)} %param.11, f32[2,32,512]{2,1,0:T(8,128)} %param.10, f32[2,32,512]{2,1,0:T(8,128)} %param.9), kind=kLoop, calls=%fused_computation | loop fusion | flops 344064 | bytes 917504 | tf_op jit(solution)/shard_map/concatenate | solution.py:642
  1.8 0.0 copy-start.3
  1.8 0.5 collective-permute-start
  2.3 0.7 %collective-permute-start.1 = (f32[7,32,512]{2,1,0:T(8,128)S(1)}, f32[7,32,512]{2,1,0:T(8,128)S(1)}, u32[]{:S(2)}, u32[]{:S(2)}) collective-permute-start(f32[7,32,512]{2,1,0:T(8,128)S(1)} %pad_maximum_fusion.refs_0_.refs_3_), channel_id=1, source_target_pairs={{8,16},{16,8},{9,17},{17,9},{10,18},{18,10},{11,19},{19,11},{12,20... | collective-permute-start | bytes 1376264 | tf_op jit(solution)/shard_map/ppermute | solution.py:25
  3.0 0.0 copy-done.1
  3.0 0.0 copy-done.4
  3.0 0.0 copy-done.3
  3.1 0.0 copy-start
  3.1 1.2 %copy-done = f32[2,512,256]{2,1,0:T(8,128)S(1)} copy-done((f32[2,512,256]{2,1,0:T(8,128)S(1)}, f32[2,512,256]{2,1,0:T(8,128)}, u32[]{:S(2)}) %copy-start) | copy-done | bytes 1048600
  4.3 1.9 %row_sums.1 = f32[32,16,128]{2,1,0:T(8,128)} custom-call(f32[2,512,256]{2,1,0:T(8,128)S(1)} %copy-done, f32[512,256]{1,0:T(8,128)S(1)} %copy-done.1, s32[1,512]{1,0:T(1,128)S(1)} %bitcast.12, s32[1,512]{1,0:T(1,128)S(1)} %bitcast.13), custom_call_target="tpu_custom_call" | custom-call | flops 4000000 | bytes 80000000 | tf_op jit(solution)/shard_map/row_sums/pallas_call | solution.py:125
  6.2 8.7 %all-to-all-start = ((f32[32,16,128]{2,1,0:T(8,128)}), f32[32,16,128]{2,1,0:T(8,128)S(1)}, u32[]{:S(2)}, u32[]{:S(2)}) async-start(f32[32,16,128]{2,1,0:T(8,128)} %row_sums.1), calls=%async_computation | async-start | bytes 524288 | tf_op jit(solution)/shard_map/all_to_all | solution.py:645
  14.9 0.0 collective-permute-done.refs_1_.refs_4_
  14.9 0.0 collective-permute-done.1.refs_2_.refs_5_
  14.9 0.2 edges.1
  15.1 1.8 %collective-permute-start.2 = (f32[7,24,128]{2,1,0:T(8,128)S(1)}, f32[7,24,128]{2,1,0:T(8,128)S(1)}, u32[]{:S(2)}, u32[]{:S(2)}) collective-permute-start(f32[7,24,128]{2,1,0:T(8,128)S(1)} %get-tuple-element.8), channel_id=1, source_target_pairs={{0,1},{2,3},{4,5},{6,7},{1,0},{3,2},{5,4},{7,6},{8,9},{10,11},{12,... | collective-permute-start | bytes 258056 | tf_op jit(solution)/shard_map/ppermute | solution.py:25
  17.0 0.7 %collective-permute-start.3 = (f32[7,24,128]{2,1,0:T(8,128)S(1)}, f32[7,24,128]{2,1,0:T(8,128)S(1)}, u32[]{:S(2)}, u32[]{:S(2)}) collective-permute-start(f32[7,24,128]{2,1,0:T(8,128)S(1)} %get-tuple-element.9), channel_id=1, source_target_pairs={{1,2},{3,4},{5,6},{2,1},{4,3},{6,5},{9,10},{11,12},{13,14},{10,9},... | collective-permute-start | bytes 258056 | tf_op jit(solution)/shard_map/ppermute | solution.py:25
  17.7 0.0 copy-start.2
  17.7 7.9 %all-to-all-done.refs_0_ = f32[32,16,128]{2,1,0:T(8,128)S(1)} async-done(((f32[32,16,128]{2,1,0:T(8,128)}), f32[32,16,128]{2,1,0:T(8,128)S(1)}, u32[]{:S(2)}, u32[]{:S(2)}) %all-to-all-start) | async-done | bytes 262176 | tf_op jit(solution)/shard_map/all_to_all | solution.py:645
  25.5 2.4 %add_on_nodes.1 = (f32[5,64,512]{2,1,0:T(8,128)S(1)}, f32[5,64,128]{2,1,0:T(8,128)S(1)}) custom-call(f32[32,16,128]{2,1,0:T(8,128)S(1)} %all-to-all-done.refs_0_), custom_call_target="tpu_custom_call" | custom-call | flops 4000000 | bytes 4000000 | tf_op jit(solution)/shard_map/add_on_nodes/pallas_call | solution.py:207
  27.9 0.0 collective-permute-done.2.refs_3_
  27.9 0.0 collective-permute-done.3.refs_4_
  27.9 0.0 copy-done.2
  28.0 16.3 %solve.1 = (f32[2,32,512]{2,1,0:T(8,128)}, f32[8,128]{1,0:T(8,128)S(1)}) custom-call(f32[7,32,512]{2,1,0:T(8,128)S(1)} %pad_maximum_fusion.refs_0_.refs_3_, f32[7,32,512]{2,1,0:T(8,128)S(1)} %collective-permute-done.refs_1_.refs_4_, f32[7,32,512]{2,1,0:T(8,128)S(1)} %collective-permute-done.1.refs_2_.refs_5_, ...), custom_call_target="tpu_custom_call" | custom-call | flops 80000000 | bytes 4000000 | tf_op jit(solution)/shard_map/solve/pallas_call | solution.py:579
  44.3 1.5 %collective-permute-start.4 = (f32[4,128]{1,0:T(4,128)S(1)}, f32[4,128]{1,0:T(4,128)S(1)}, u32[]{:S(2)}, u32[]{:S(2)}) collective-permute-start(f32[4,128]{1,0:T(4,128)S(1)} %bitcast.18), channel_id=1, source_target_pairs={{0,1},{1,0},{2,3},{3,2},{4,5},{5,4},{6,7},{7,6},{8,9},{9,8},{10,11... | collective-permute-start | bytes 6152 | tf_op jit(solution)/shard_map/ppermute | solution.py:621
  45.7 2.2 %collective-permute-done.4 = f32[4,128]{1,0:T(4,128)S(1)} collective-permute-done((f32[4,128]{1,0:T(4,128)S(1)}, f32[4,128]{1,0:T(4,128)S(1)}, u32[]{:S(2)}, u32[]{:S(2)}) %collective-permute-start.4) | collective-permute-done | bytes 2080 | tf_op jit(solution)/shard_map/ppermute | solution.py:621
  47.9 1.0 %collective-permute-start.5 = (f32[2,128]{1,0:T(2,128)S(1)}, f32[2,128]{1,0:T(2,128)S(1)}, u32[]{:S(2)}, u32[]{:S(2)}) collective-permute-start(f32[2,128]{1,0:T(2,128)S(1)} %bitcast.19), channel_id=1, source_target_pairs={{0,2},{1,3},{2,0},{3,1},{4,6},{5,7},{6,4},{7,5},{8,10},{9,11},{10,... | collective-permute-start | bytes 3080 | tf_op jit(solution)/shard_map/ppermute | solution.py:621
  48.9 2.6 %collective-permute-done.5 = f32[2,128]{1,0:T(2,128)S(1)} collective-permute-done((f32[2,128]{1,0:T(2,128)S(1)}, f32[2,128]{1,0:T(2,128)S(1)}, u32[]{:S(2)}, u32[]{:S(2)}) %collective-permute-start.5) | collective-permute-done | bytes 1056 | tf_op jit(solution)/shard_map/ppermute | solution.py:621
  51.6 0.6 %collective-permute-start.6 = (f32[1,128]{1,0:T(1,128)S(1)}, f32[1,128]{1,0:T(1,128)S(1)}, u32[]{:S(2)}, u32[]{:S(2)}) collective-permute-start(f32[1,128]{1,0:T(1,128)S(1)} %constant_dynamic-slice_fusion), channel_id=1, source_target_pairs={{0,4},{1,5},{2,6},{3,7},{4,0},{5,1},{6,2},{7,3},{8,12},{9,13},{10,... | collective-permute-start | bytes 1544 | tf_op jit(solution)/shard_map/ppermute | solution.py:621
  52.2 3.9 %collective-permute-done.6 = f32[1,128]{1,0:T(1,128)S(1)} collective-permute-done((f32[1,128]{1,0:T(1,128)S(1)}, f32[1,128]{1,0:T(1,128)S(1)}, u32[]{:S(2)}, u32[]{:S(2)}) %collective-permute-start.6) | collective-permute-done | bytes 544 | tf_op jit(solution)/shard_map/ppermute | solution.py:621
  56.1 0.5 fusion.1
  (5 shorter events, 0.0 us)
Async XLA Ops:
  0.6 2.4 %copy-start.1 = (f32[512,256]{1,0:T(8,128)S(1)}, f32[512,256]{1,0:T(8,128)}, u32[]{:S(2)}) copy-start(f32[512,256]{1,0:T(8,128)} %refs_1_.1) | copy-start | bytes 1572868
  0.6 2.4 %copy-start.4 = (s32[512]{0:T(512)S(1)}, s32[512]{0:T(512)}, u32[]{:S(2)}) copy-start(s32[512]{0:T(512)} %param.17) | copy-start | bytes 6148
  1.8 1.2 %copy-start.3 = (s32[512,1]{0,1:T(1,128)S(1)}, s32[512,1]{0,1:T(1,128)}, u32[]{:S(2)}) copy-start(s32[512,1]{0,1:T(1,128)} %param.16) | copy-start | bytes 6148
  1.8 13.1 %collective-permute-start = (f32[7,32,512]{2,1,0:T(8,128)S(1)}, f32[7,32,512]{2,1,0:T(8,128)S(1)}, u32[]{:S(2)}, u32[]{:S(2)}) collective-permute-start(f32[7,32,512]{2,1,0:T(8,128)S(1)} %pad_maximum_fusion.refs_0_.refs_3_), channel_id=1, source_target_pairs={{0,8},{16,24},{8,0},{24,16},{1,9},{17,25},{9,1},{25,17},{2,10},{18... | collective-permute-start | bytes 1376264 | tf_op jit(solution)/shard_map/ppermute | solution.py:25
  2.3 12.6 %collective-permute-start.1 = (f32[7,32,512]{2,1,0:T(8,128)S(1)}, f32[7,32,512]{2,1,0:T(8,128)S(1)}, u32[]{:S(2)}, u32[]{:S(2)}) collective-permute-start(f32[7,32,512]{2,1,0:T(8,128)S(1)} %pad_maximum_fusion.refs_0_.refs_3_), channel_id=1, source_target_pairs={{8,16},{16,8},{9,17},{17,9},{10,18},{18,10},{11,19},{19,11},{12,20... | collective-permute-start | bytes 1376264 | tf_op jit(solution)/shard_map/ppermute | solution.py:25
  3.1 1.2 %copy-start = (f32[2,512,256]{2,1,0:T(8,128)S(1)}, f32[2,512,256]{2,1,0:T(8,128)}, u32[]{:S(2)}) copy-start(f32[2,512,256]{2,1,0:T(8,128)} %refs_0_.1) | copy-start | bytes 3145732
  6.2 19.4 %all-to-all-start = ((f32[32,16,128]{2,1,0:T(8,128)}), f32[32,16,128]{2,1,0:T(8,128)S(1)}, u32[]{:S(2)}, u32[]{:S(2)}) async-start(f32[32,16,128]{2,1,0:T(8,128)} %row_sums.1), calls=%async_computation | async-start | bytes 524288 | tf_op jit(solution)/shard_map/all_to_all | solution.py:645
  15.1 12.8 %collective-permute-start.2 = (f32[7,24,128]{2,1,0:T(8,128)S(1)}, f32[7,24,128]{2,1,0:T(8,128)S(1)}, u32[]{:S(2)}, u32[]{:S(2)}) collective-permute-start(f32[7,24,128]{2,1,0:T(8,128)S(1)} %get-tuple-element.8), channel_id=1, source_target_pairs={{0,1},{2,3},{4,5},{6,7},{1,0},{3,2},{5,4},{7,6},{8,9},{10,11},{12,... | collective-permute-start | bytes 258056 | tf_op jit(solution)/shard_map/ppermute | solution.py:25
  17.0 11.0 %collective-permute-start.3 = (f32[7,24,128]{2,1,0:T(8,128)S(1)}, f32[7,24,128]{2,1,0:T(8,128)S(1)}, u32[]{:S(2)}, u32[]{:S(2)}) collective-permute-start(f32[7,24,128]{2,1,0:T(8,128)S(1)} %get-tuple-element.9), channel_id=1, source_target_pairs={{1,2},{3,4},{5,6},{2,1},{4,3},{6,5},{9,10},{11,12},{13,14},{10,9},... | collective-permute-start | bytes 258056 | tf_op jit(solution)/shard_map/ppermute | solution.py:25
  17.7 10.3 %copy-start.2 = (s32[32,512]{1,0:T(8,128)S(1)}, s32[32,512]{1,0:T(8,128)}, u32[]{:S(2)}) copy-start(s32[32,512]{1,0:T(8,128)} %refs_7_.1) | copy-start | bytes 196612
  44.3 3.7 %collective-permute-start.4 = (f32[4,128]{1,0:T(4,128)S(1)}, f32[4,128]{1,0:T(4,128)S(1)}, u32[]{:S(2)}, u32[]{:S(2)}) collective-permute-start(f32[4,128]{1,0:T(4,128)S(1)} %bitcast.18), channel_id=1, source_target_pairs={{0,1},{1,0},{2,3},{3,2},{4,5},{5,4},{6,7},{7,6},{8,9},{9,8},{10,11... | collective-permute-start | bytes 6152 | tf_op jit(solution)/shard_map/ppermute | solution.py:621
  47.9 3.6 %collective-permute-start.5 = (f32[2,128]{1,0:T(2,128)S(1)}, f32[2,128]{1,0:T(2,128)S(1)}, u32[]{:S(2)}, u32[]{:S(2)}) collective-permute-start(f32[2,128]{1,0:T(2,128)S(1)} %bitcast.19), channel_id=1, source_target_pairs={{0,2},{1,3},{2,0},{3,1},{4,6},{5,7},{6,4},{7,5},{8,10},{9,11},{10,... | collective-permute-start | bytes 3080 | tf_op jit(solution)/shard_map/ppermute | solution.py:621
  51.6 4.5 %collective-permute-start.6 = (f32[1,128]{1,0:T(1,128)S(1)}, f32[1,128]{1,0:T(1,128)S(1)}, u32[]{:S(2)}, u32[]{:S(2)}) collective-permute-start(f32[1,128]{1,0:T(1,128)S(1)} %constant_dynamic-slice_fusion), channel_id=1, source_target_pairs={{0,4},{1,5},{2,6},{3,7},{4,0},{5,1},{6,2},{7,3},{8,12},{9,13},{10,... | collective-permute-start | bytes 1544 | tf_op jit(solution)/shard_map/ppermute | solution.py:621
